TPU v7x, 128 devices: a whole 4x4x4 slice. The times are simulated.
128 devices in a mesh: seq: 16 (over x_hi, z, core), blk: 8 (over y, x_lo).
Axes of the slice: x: 4 (x_hi: 2, x_lo: 2; x = x_hi * 2 + x_lo), y: 4, z: 4, core: 2. Of those that a mesh axis runs over, the one named last changes fastest.
Arguments:
- tokens: bfloat16 [16384, 3072], P(('seq', 'blk')), may hold values from -8.6 to 8.6
- project_weight: bfloat16 [3, 3072, 2048], P(None, None, 'seq')
- noisy_latent: float32 [16384, 64], P(('seq', 'blk')), may hold values from -6 to 6
- final_weight: bfloat16 [2048, 64], replicated, may hold values from -0.5 to 0.5
- conv_weight: bfloat16 [432, 512], replicated, may hold values from -0.3125 to 0.3125
- norm_gain: float32 [512], replicated, may hold values from 0.1 to 1.9
- norm_shift: float32 [512], replicated, may hold values from -3 to 3
- owner_count: int32 [128], replicated, may hold values from 1 to 4, 256 in all
- intersection: int32 [256, 4], replicated, may hold values from 0 to 127, as said below
Outputs:
- decoded: bfloat16 [128, 4, 512, 2048], P(('seq', 'blk'))
Inputs may be any that keep to these rules, and one draw needn't show every extreme that they name: Owner o holds pixel tiles s to s + owner_count[o] - 1, s the sum of the counts below o; the counts sum to 256 and one owner holds exactly 4. `intersection`: row p names the four latent tiles of a 2 x 2 block of neighbouring tiles on a grid of 16 rows by 8 columns, tile r * 8 + c at row r, column c, in the order top left, top right, bottom left, bottom right.
All inputs are finite; a program needn't handle non-finite values.
Results may differ from a plain program's by a relative error of at most 0.014.
Values may be sent and summed in bfloat16 or wider, within the bound.
No kernel may reach another device: no remote copies, remote signals or barrier semaphores. Data moves between devices by JAX's collectives and lax.ppermute only.
A program may use at most 128 MiB of HBM per device.

v0:
```python
import functools

import jax
import jax.numpy as jnp
import numpy as np
from jax import lax
from jax.experimental import pallas as pl
from jax.experimental.pallas import tpu as pltpu
from jax.sharding import Mesh
from jax.sharding import PartitionSpec as P

HEAD_DIM = 128
LATENT_CH = 16
PATCH = 4
GROUPS = 32
MAXPIX = 4
PARTS = 2

scale_factor = 0.476986
step_size = 0.25
norm_eps = 1e-06

AXES = ("xh", "z", "c", "y", "xl")
SIZES = (2, 4, 2, 4, 2)
SEQ = ("xh", "z", "c")

NT = (((1,), (1,)), ((), ()))
LOG2E = 1.4426950408889634
PAYLOAD = 80


def shift(x, **moves):
    pairs = []
    for source in range(int(np.prod(SIZES))):
        place = np.unravel_index(source, SIZES)
        target = [(p + moves.get(a, 0)) % n for p, a, n in zip(place, AXES, SIZES)]
        pairs.append((source, int(np.ravel_multi_index(target, SIZES))))
    return lax.ppermute(x, AXES, pairs)


def regroup_kernel(places, n_after, *refs):
    in_refs, out_refs = refs[: len(places)], refs[len(places) + n_after :]
    for in_ref, (out, target) in zip(in_refs, places):
        out_refs[out][target : target + in_ref.shape[0], :] = in_ref[...]


def regroup(groups, after=(), small=(), block=32):
    operands, in_specs, places, shapes = [], [], [], []
    for out, pieces in enumerate(groups):
        target = 0
        for x, start, rows, *columns in pieces:
            column, width = columns or (0, x.shape[1])
            for row in range(start, start + rows, block):
                operands.append(x)
                in_specs.append(
                    pl.BlockSpec((block, width), lambda i, n=row // block, c=column: (n, c))
                )
                places.append((out, target))
                target += block
        shapes.append(jax.ShapeDtypeStruct((target, width), pieces[0][0].dtype))
    return pl.pallas_call(
        functools.partial(regroup_kernel, places, len(after) + len(small)),
        grid=(1,),
        in_specs=in_specs
        + [pl.BlockSpec(memory_space=pltpu.HBM)] * len(after)
        + [pl.BlockSpec(memory_space=pltpu.VMEM)] * len(small),
        out_specs=[pl.BlockSpec(shape.shape, lambda i: (0, 0)) for shape in shapes],
        out_shape=shapes,
        compiler_params=pltpu.CompilerParams(vmem_limit_bytes=20 << 20),
        name="regroup",
    )(*operands, *after, *small)


def project_kernel(q_order, scale, n_after, *refs):
    sources, (own_w_ref, other_w_ref, *refs) = refs[:4], refs[4:]
    q_ref, kv_ref, sent_ref, x_ref, w_ref, sem = refs[n_after:]
    rows = sources[0].shape[0]
    copies = [
        pltpu.make_async_copy(ref, x_ref.at[pl.ds(n * rows, rows), :], sem.at[n])
        for n, ref in enumerate(sources)
    ]
    for copy in copies:
        copy.start()
    for i in range(3):
        for n, weights in enumerate((own_w_ref, other_w_ref)):
            column = (3 * n + i) * HEAD_DIM
            w_ref[:, column : column + HEAD_DIM] = weights[i]
    for first in range(0, 4 * rows, 2 * rows):
        for copy in copies[first // rows : first // rows + 2]:
            copy.wait()
        out = jnp.dot(
            x_ref[first : first + 2 * rows, :], w_ref[...], preferred_element_type=jnp.float32
        )
        own_q = (out[:, :HEAD_DIM] * scale).astype(jnp.bfloat16)
        sent_q = (out[:, 3 * HEAD_DIM : 4 * HEAD_DIM] * scale).astype(jnp.bfloat16)
        for start, count, target in q_order:
            if first <= start < first + 2 * rows:
                piece, target = slice(start - first, start - first + count), slice(target, target + count)
                q_ref[target, :] = own_q[piece]
                sent_ref[target, 2 * HEAD_DIM :] = sent_q[piece]
        piece = slice(first, first + 2 * rows)
        kv_ref[piece, :] = out[:, HEAD_DIM : 3 * HEAD_DIM].astype(jnp.bfloat16)
        sent_ref[piece, : 2 * HEAD_DIM] = out[:, 4 * HEAD_DIM :].astype(jnp.bfloat16)


def project(xs, own_weight, other_weight, q_order, scale, after=()):
    rows, depth = 4 * xs[0].shape[0], own_weight.shape[1]
    widths = [HEAD_DIM, 2 * HEAD_DIM, 3 * HEAD_DIM]
    anywhere, vmem = pl.BlockSpec(memory_space=pltpu.HBM), pl.BlockSpec(memory_space=pltpu.VMEM)
    return pl.pallas_call(
        functools.partial(project_kernel, q_order, scale, len(after)),
        in_specs=[anywhere] * 4 + [vmem] * 2 + [anywhere] * len(after),
        out_specs=[vmem] * 3,
        out_shape=[jax.ShapeDtypeStruct((rows, width), jnp.bfloat16) for width in widths],
        scratch_shapes=[
            pltpu.VMEM((rows, depth), jnp.bfloat16),
            pltpu.VMEM((depth, 6 * HEAD_DIM), jnp.bfloat16),
            pltpu.SemaphoreType.DMA((4,)),
        ],
        compiler_params=pltpu.CompilerParams(vmem_limit_bytes=40 << 20),
        name="project",
    )(*xs, own_weight, other_weight, *after)


def softmax_blocks(q, kv_refs, value_ref, bk, run_max, acc):
    places, start = [], 0
    for ref in kv_refs:
        for i in range(0, ref.shape[0], bk):
            places.append((ref, i, start + i))
        start += ref.shape[0]

    def scores_of(n):
        ref, i, _ = places[n]
        return lax.dot_general(
            q, ref[i : i + bk, :HEAD_DIM], NT, preferred_element_type=jnp.float32
        )

    following = scores_of(0)
    for n, (_, _, row) in enumerate(places):
        scores = following
        if n + 1 < len(places):
            following = scores_of(n + 1)
        new_max = jnp.max(scores, axis=1, keepdims=True)
        if run_max is not None:
            new_max = jnp.maximum(run_max, new_max)
        probs = jnp.exp2(scores - new_max).astype(jnp.bfloat16)
        part = jnp.dot(probs, value_ref[row : row + bk, :], preferred_element_type=jnp.float32)
        acc = part if acc is None else acc * jnp.exp2(run_max - new_max) + part
        run_max = new_max
    return run_max, acc


def attention_kernel(bk, n_q, n_kv, carry_in, n_into, final, *refs):
    if final:
        place_ref, *refs = refs
    q_refs, refs = refs[:n_q], refs[n_q:]
    kv_refs, refs = refs[:n_kv], refs[n_kv:]
    if carry_in:
        acc_in_ref, max_in_ref, *refs = refs
    refs = refs[n_into:]
    if final:
        w_ref, out_ref, value_ref = refs
    else:
        acc_out_ref, max_out_ref, value_ref = refs

    @pl.when(pl.program_id(0) == 0)
    def _():
        start = 0
        for ref in kv_refs:
            n = ref.shape[0]
            value_ref[start : start + n, :HEAD_DIM] = ref[:, HEAD_DIM:]
            value_ref[start : start + n, HEAD_DIM:] = jnp.ones((n, HEAD_DIM), jnp.bfloat16)
            start += n

    q = q_refs[0][...]
    for n in range(1, n_q):
        q = jnp.where(pl.program_id(0) == n, q_refs[n][...], q)
    bq = q.shape[0]
    run_max, acc = None, None
    if carry_in:
        run_max, acc = jnp.max(max_in_ref[...], axis=1, keepdims=True), acc_in_ref[...]
    run_max, acc = softmax_blocks(q, kv_refs, value_ref, bk, run_max, acc)
    if not final:
        acc_out_ref[...] = acc
        max_out_ref[...] = jnp.broadcast_to(run_max, max_out_ref.shape)
        return

    total = acc[:, HEAD_DIM:]
    attended = (acc[:, :HEAD_DIM] / total).astype(jnp.bfloat16)
    velocity = lax.dot_general(w_ref[...], attended, NT, preferred_element_type=jnp.float32)
    log_sum = run_max + jnp.log2(total)
    high = log_sum.astype(jnp.bfloat16).astype(jnp.float32)
    mid = (log_sum - high).astype(jnp.bfloat16).astype(jnp.float32)
    low = log_sum - high - mid
    lane = lax.broadcasted_iota(jnp.int32, (bq, HEAD_DIM), 1)
    terms = jnp.where(lane == 0, high, jnp.where(lane == 1, mid, low)).astype(jnp.bfloat16)
    row = lax.broadcasted_iota(jnp.int32, (PAYLOAD - 64, HEAD_DIM), 0)
    column = lax.broadcasted_iota(jnp.int32, (PAYLOAD - 64, HEAD_DIM), 1)
    pick = ((row == column) & (row < 3)).astype(jnp.float32).astype(jnp.bfloat16)
    stats = lax.dot_general(pick, terms, NT, preferred_element_type=jnp.float32)
    joined = jnp.concatenate([velocity, stats], axis=0).astype(jnp.bfloat16)
    n_xh, n_z, n_c = out_ref.shape[:3]
    late = pl.program_id(0) % 2
    for core in range(n_c):
        for group, (early_place, late_place) in enumerate(zip(*GROUP_PLACES)):
            t = core * len(GROUP_PLACES[0]) + group
            xh, z = [jnp.where(late == 1, q, p) for p, q in zip(early_place, late_place)]
            out_ref[
                (xh + place_ref[1]) % n_xh, (z + place_ref[2]) % n_z, (core + place_ref[3]) % n_c, 0
            ] = joined[:, t * 128 : (t + 1) * 128]


GROUP_PLACES = (((0, 0), (0, 3), (0, 1), (1, 0)), ((0, 2), (1, 3), (1, 1), (1, 2)))


def attention(qs, kvs, carry=None, fresh=False, blocks=(1, 0), last=None, bk=512):
    bq = qs[0].shape[0]
    length = sum(kv.shape[0] for kv in kvs)
    stride, offset = blocks
    widths = (2 * HEAD_DIM, HEAD_DIM)
    whole = lambda x: pl.BlockSpec(x.shape, lambda i, *p: (0, 0))
    carried = [
        pl.BlockSpec((bq, width), lambda i, *p: (i * stride + offset, 0)) for width in widths
    ]
    operands = [*qs, *kvs]
    in_specs = [whole(x) for x in operands]
    aliases = {}
    if carry is not None:
        if last is None:
            aliases = {len(operands): 0, len(operands) + 1: 1}
        operands += carry
        in_specs += [pl.BlockSpec(memory_space=pltpu.HBM)] * 2 if fresh else carried
    if last is None:
        prefetch = []
        out_specs = carried
        out_shape = [jax.ShapeDtypeStruct((4 * bq, width), jnp.float32) for width in widths]
    else:
        prefetch = [last[0]]
        operands.append(last[1])
        in_specs.append(whole(last[1]))
        out_specs = pl.BlockSpec(
            (2, 4, 2, 1, PAYLOAD, 128), lambda i, p: (0, 0, 0, (i // 2 + p[0]) % 2, 0, 0)
        )
        out_shape = jax.ShapeDtypeStruct((2, 4, 2, 2, PAYLOAD, 128), jnp.bfloat16)
    read = carry is not None and not fresh
    return pl.pallas_call(
        functools.partial(
            attention_kernel, bk, len(qs), len(kvs), read, len(aliases) if fresh else 0, last is not None
        ),
        grid_spec=pltpu.PrefetchScalarGridSpec(
            num_scalar_prefetch=len(prefetch),
            grid=(len(qs),),
            in_specs=in_specs,
            out_specs=out_specs,
            scratch_shapes=[pltpu.VMEM((length, 2 * HEAD_DIM), jnp.bfloat16)],
        ),
        out_shape=out_shape,
        input_output_aliases=aliases,
        compiler_params=pltpu.CompilerParams(vmem_limit_bytes=56 << 20),
        name="attention",
    )(*prefetch, *operands)


def combine_kernel(parts_ref, noisy_ref, out_ref):
    velocity = jnp.zeros((64, 128), jnp.float32)
    for head in range(parts_ref.shape[0] // 2):
        logs = []
        for half in range(2):
            terms = parts_ref[2 * head + half, 64:PAYLOAD, :].astype(jnp.float32)
            logs.append(terms[0:1] + terms[1:2] + terms[2:3])
        top = jnp.maximum(logs[0], logs[1])
        first, second = jnp.exp2(logs[0] - top), jnp.exp2(logs[1] - top)
        inverse = 1.0 / (first + second)
        velocity += parts_ref[2 * head, 0:64, :].astype(jnp.float32) * (first * inverse)
        velocity += parts_ref[2 * head + 1, 0:64, :].astype(jnp.float32) * (second * inverse)
    latent = (noisy_ref[...] - step_size * velocity) / scale_factor
    latent = latent.astype(jnp.bfloat16)
    for n in range(out_ref.shape[0]):
        out_ref[n] = latent


def combine(parts, noisy, copies):
    return pl.pallas_call(
        combine_kernel,
        out_shape=jax.ShapeDtypeStruct((copies, 64, 128), jnp.bfloat16),
        name="latent_tile",
    )(parts, noisy)


def placing_matrix():
    side, p, q, i, j = np.meshgrid(*[np.arange(n) for n in (2, 2, 2, 8, 8)], indexing="ij")
    target = (2 * i + p) * 32 + side * 16 + 2 * j + q
    place = np.zeros((512, 512), np.float32)
    place[np.arange(512), target.reshape(-1)] = 1.0
    return place


def decode_kernel(
    ids_ref, own_ref, other_ref, place_ref, first_ref, second_ref, gain_ref, shift_ref, out_ref, wide_ref, half_ref, patch_ref, conv_ref, part_ref, mean_ref, scale_ref, mid_ref
):
    slot, part = pl.program_id(0), pl.program_id(1)
    channels, voxels = conv_ref.shape
    these = pl.ds(pl.multiple_of(part * channels, channels), channels)

    @pl.when((slot == 0) & (part == 0))
    def _():
        for s in range(MAXPIX):
            for half in range(2):
                for side in range(2):
                    n = ids_ref[1 + s * 4 + half * 2 + side]
                    tile = jnp.where(n < 64, own_ref[n % 64], other_ref[n % 64])
                    for pq in range(4):
                        column = (side * 4 + pq) * 64
                        for f in range(2):
                            row = ((s * 2 + f) * 2 + half) * 16
                            wide_ref[row : row + 16, column : column + 64] = tile[
                                pq * 16 : pq * 16 + 16, f * 64 : f * 64 + 64
                            ]
        half_ref[...] = jnp.dot(wide_ref[...], place_ref[...], preferred_element_type=jnp.float32)

    @pl.when(slot >= ids_ref[0])
    def _():
        out_ref[...] = jnp.zeros(out_ref.shape, out_ref.dtype)

    @pl.when((slot < ids_ref[0]) & (part == 0))
    def _():
        halves = half_ref[pl.ds(pl.multiple_of(slot * 64, 64), 64), :]
        region = jnp.concatenate(
            [
                jnp.concatenate([halves[0:16], halves[16:32]], axis=1),
                jnp.concatenate([halves[32:48], halves[48:64]], axis=1),
            ],
            axis=0,
        )
        lane = lax.broadcasted_iota(jnp.int32, region.shape, 1)
        column = lane % 32
        for g in range(3):
            if g == 0:
                across = jnp.where(column == 0, region, pltpu.roll(region, 1, 1))
            elif g == 1:
                across = region
            else:
                across = jnp.where(column == 31, region, pltpu.roll(region, 1023, 1))
            for b in range(3):
                if b == 0:
                    tap = jnp.where(lane < 32, across, pltpu.roll(across, 32, 1))
                elif b == 1:
                    tap = across
                else:
                    tap = jnp.where(lane >= 992, across, pltpu.roll(across, 992, 1))
                row = (b * 3 + g) * 16
                tap = tap.astype(jnp.bfloat16)
                patch_ref[row : row + 16, :] = tap[0:16]
                patch_ref[144 + row : 144 + row + 16, :] = tap[16:32]
    @pl.when(slot < ids_ref[0])
    def _():
        conv_ref[:, :1024] = jnp.dot(
            first_ref[these, :], patch_ref[0:144, :], preferred_element_type=jnp.float32
        )
        conv_ref[:, 1024:] = jnp.dot(
            second_ref[these, :], patch_ref[...], preferred_element_type=jnp.float32
        )
        groups = GROUPS // PARTS
        size = channels // groups
        count = 1.0 / (size * voxels)

        def group_rows(group):
            return slice(group * size, (group + 1) * size)

        def group_means():
            sums = jnp.sum(part_ref[...], axis=1, keepdims=True)
            sums = jnp.sum(sums.reshape(groups, 8, 1), axis=1, keepdims=True) * count
            return jnp.broadcast_to(sums, (groups, size, 128)).reshape(channels, 128)

        for group in range(groups):
            total = jnp.zeros((size, 128), jnp.float32)
            for j in range(0, voxels, 128):
                total += conv_ref[group_rows(group), j : j + 128]
            part_ref[group * 8 : group * 8 + 8, :] = total[:8] + total[8:]
        mean_ref[...] = group_means()
        for group in range(groups):
            mean = mean_ref[group_rows(group), :]
            total = jnp.zeros((size, 128), jnp.float32)
            for j in range(0, voxels, 128):
                apart = conv_ref[group_rows(group), j : j + 128] - mean
                total += apart * apart
            part_ref[group * 8 : group * 8 + 8, :] = total[:8] + total[8:]
        scale_ref[...] = gain_ref[these, :] * (lax.rsqrt(group_means() + norm_eps) * 0.5)
        mid_ref[...] = jnp.broadcast_to(shift_ref[these, :] * 0.5, mid_ref.shape)
        for group in range(groups):
            rows = group_rows(group)
            mean, scale = mean_ref[rows, :], scale_ref[rows, :]
            half_shift = mid_ref[rows, :]
            for j in range(0, voxels, 128):
                half_norm = (conv_ref[rows, j : j + 128] - mean) * scale + half_shift
                out_ref[0, 0, rows, j : j + 128] = (
                    half_norm + half_norm * jnp.tanh(half_norm)
                ).astype(jnp.bfloat16)


def decode(ids, own_tiles, other_tiles, place, first, second, gain, shift_rows):
    channels = first.shape[0]
    whole = lambda shape: pl.BlockSpec(memory_space=pltpu.VMEM)
    rows = channels // PARTS
    return pl.pallas_call(
        decode_kernel,
        grid_spec=pltpu.PrefetchScalarGridSpec(
            num_scalar_prefetch=1,
            grid=(MAXPIX, PARTS),
            in_specs=[
                whole(own_tiles.shape),
                whole(other_tiles.shape),
                whole(place.shape),
                whole(first.shape),
                whole(second.shape),
                whole(gain.shape),
                whole(shift_rows.shape),
            ],
            out_specs=pl.BlockSpec((1, 1, rows, 2048), lambda s, h, ids: (0, s, h, 0)),
            scratch_shapes=[
                pltpu.VMEM((256, 512), jnp.bfloat16),
                pltpu.VMEM((256, 512), jnp.float32),
                pltpu.VMEM((288, 1024), jnp.bfloat16),
                pltpu.VMEM((rows, 2048), jnp.float32),
                pltpu.VMEM((GROUPS // PARTS * 8, 128), jnp.float32),
                pltpu.VMEM((rows, 128), jnp.float32),
                pltpu.VMEM((rows, 128), jnp.float32),
                pltpu.VMEM((rows, 128), jnp.float32),
            ],
        ),
        out_shape=jax.ShapeDtypeStruct((1, MAXPIX, channels, 2048), jnp.bfloat16),
        compiler_params=pltpu.CompilerParams(vmem_limit_bytes=28 << 20),
        name="decode",
    )(ids, own_tiles, other_tiles, place, first, second, gain, shift_rows)


def body(
    tokens,
    project_weight,
    noisy_latent,
    final_weight,
    conv_weight,
    norm_gain,
    norm_shift,
    owner_count,
    intersection,
):
    coordinate = {axis: lax.axis_index(axis).astype(jnp.int32) for axis in AXES}
    head = lax.axis_index(SEQ)

    w = lax.dynamic_slice_in_dim(final_weight, head * HEAD_DIM, HEAD_DIM, axis=0)
    w = w.reshape(HEAD_DIM, LATENT_CH, PATCH).transpose(2, 1, 0).reshape(64, HEAD_DIM)
    noisy = noisy_latent.reshape(-1, LATENT_CH, PATCH).transpose(2, 1, 0).reshape(64, -1)

    rank = lax.axis_index(AXES)
    ends = jnp.cumsum(owner_count, dtype=jnp.int32)
    count = owner_count[rank]
    slots = jnp.minimum(ends[rank] - count + jnp.arange(MAXPIX), intersection.shape[0] - 1)
    wanted = intersection[slots].reshape(-1)
    core = (wanted // 8) % 2
    wanted = (wanted // 16) * 8 + wanted % 8 + 64 * (core != coordinate["c"])
    ids = jnp.concatenate([count[None], wanted]).astype(jnp.int32)

    taps = conv_weight.astype(jnp.float32).reshape(3, -1, conv_weight.shape[1])
    first = (taps[0] + taps[1] + taps[2]).T.astype(jnp.bfloat16)
    second = jnp.concatenate([taps[0] + taps[1], taps[2]], axis=0).T.astype(jnp.bfloat16)
    placing = jnp.asarray(placing_matrix(), jnp.bfloat16)
    decoder = [first, second, norm_gain[:, None], norm_shift[:, None]]

    other_weight = shift(project_weight, c=1)
    below, above, across = shift(tokens, z=1), shift(tokens, z=-1), shift(tokens, xh=1)
    opposite = shift(tokens, xh=1, z=2)
    to_above, to_below, to_across = regroup(
        [
            [(below, 0, 64), (across, 0, 32), (across, 96, 32)],
            [(across, 0, 32), (across, 96, 32), (above, 64, 64)],
            [(below, 32, 64), (above, 32, 64)],
        ],
        small=decoder[:2],
    )
    far_low, far_high, inner = shift(to_above, z=1), shift(to_below, z=-1), shift(to_across, xh=1)

    q_scale = LOG2E * HEAD_DIM**-0.5

    def join(own, received, column, width, after=(), small=()):
        rows = own.shape[0]
        pieces = [(own, 0, rows), (received, 0, rows, column, width)]
        return regroup([pieces], after, small, block=rows)[0]

    early = [tokens, below, above, across]
    early = project(early, project_weight, other_weight, [(0, 256, 0), (256, 256, 256)], q_scale, [to_above])
    received = shift(early[2], c=1)
    kv1 = [join(early[1], received, 0, 2 * HEAD_DIM)]
    kv1 += [shift(kv1[0], y=1), shift(kv1[0], y=3)]
    arrived = [*kv1[1:], far_low, far_high, inner, opposite]
    q1 = join(early[0], received, 2, HEAD_DIM)
    kv1_again = join(early[1], received, 0, 2 * HEAD_DIM, arrived, [ids, w, noisy, *decoder[2:]])
    prepared = [q1, kv1_again]
    kv1.append(shift(kv1_again, y=2))
    q1 = [q1, shift(q1, xl=1)]

    late_order = [(0, 64, 0), (64, 32, 128), (96, 32, 224)]
    late_order += [(128, 32, 256), (160, 32, 352), (192, 64, 64)]
    late_order += [(256, 64, 160), (320, 64, 288), (384, 128, 384)]
    late = [far_low, far_high, inner, opposite]
    q2, own_kv2, sent = project(late, project_weight, other_weight, late_order, q_scale, prepared)
    received = shift(sent, c=1)
    kv2 = [join(own_kv2, received, 0, 2 * HEAD_DIM)]
    kv2 += [shift(kv2[0], y=n) for n in (1, 3, 2)]
    q2 = join(q2, received, 2, HEAD_DIM)
    q2 = [q2, shift(q2, xl=1)]

    carry = attention(q1, [*kv1[:3], kv2[0]], blocks=(2, 0))
    carry = attention(q2, [*kv1[:3], kv2[0]], carry, fresh=True, blocks=(2, 1))
    q_all = [q1[0], q2[0], q1[1], q2[1]]
    place = jnp.stack([coordinate[axis] for axis in ("xl", "xh", "z", "c")])
    parts = attention(q_all, [kv1[3], *kv2[1:]], carry, last=(place, w))
    parts = parts.reshape(-1, PAYLOAD, 128)
    parts = lax.all_to_all(parts, SEQ + ("xl",), split_axis=0, concat_axis=0, tiled=True)
    tile = combine(parts, noisy, 64)

    own_tiles = lax.all_to_all(tile, ("xh", "z", "y", "xl"), split_axis=0, concat_axis=0, tiled=True)
    other_tiles = shift(own_tiles, c=1)
    return decode(ids, own_tiles, other_tiles, placing, *decoder)


def solution(mesh):
    fine = Mesh(mesh.devices.reshape(SIZES), AXES)
    blk = ("y", "xl")
    return jax.shard_map(
        body,
        mesh=fine,
        in_specs=(
            P(SEQ + blk, None),
            P(None, None, SEQ),
            P(SEQ + blk, None),
            P(),
            P(),
            P(),
            P(),
            P(),
            P(),
        ),
        out_specs=P(SEQ + blk, None, None, None),
        check_vma=False,
    )
```

profile of v0, /device:TPU:9, one launch (start us, length us, event | category | flops | bytes accessed | tf_op | source)
XLA Modules:
  0.0 196.6 jit_solution(13971241059186682169)
XLA Ops:
  0.7 1.6 collective-permute-start
  2.3 2.1 %collective-permute-start.1 = (bf16[128,3072]{1,0:T(8,128)(2,1)}, bf16[128,3072]{1,0:T(8,128)(2,1)S(1)}, u32[]{:S(2)}, u32[]{:S(2)}) collective-permute-start(bf16[128,3072]{1,0:T(8,128)(2,1)} %refs_0_.1), channel_id=1, source_target_pairs={{0,48},{1,49},{2,50},{3,51},{4,52},{5,53},{6,54},{7,55},{8,56},{9,... | collective-permute-start | bytes 2359304 | tf_op jit(solution)/shard_map/ppermute | solution.py:38
  4.4 2.7 %collective-permute-start.2 = (bf16[128,3072]{1,0:T(8,128)(2,1)}, bf16[128,3072]{1,0:T(8,128)(2,1)S(1)}, u32[]{:S(2)}, u32[]{:S(2)}) collective-permute-start(bf16[128,3072]{1,0:T(8,128)(2,1)} %refs_0_.1), channel_id=1, source_target_pairs={{0,64},{1,65},{2,66},{3,67},{4,68},{5,69},{6,70},{7,71},{8,72},{9,... | collective-permute-start | bytes 2359304 | tf_op jit(solution)/shard_map/ppermute | solution.py:38
  7.2 1.2 collective-permute-start.8
  8.4 1.2 copy.19
  10.4 12.0 %collective-permute-done.refs_0_.refs_1_.refs_8_.refs_9_ = bf16[128,3072]{1,0:T(8,128)(2,1)S(1)} collective-permute-done((bf16[128,3072]{1,0:T(8,128)(2,1)}, bf16[128,3072]{1,0:T(8,128)(2,1)S(1)}, u32[]{:S(2)}, u32[]{:S(2)}) %collective-permute-start) | collective-permute-done | bytes 786464 | tf_op jit(solution)/shard_map/ppermute | solution.py:38
  22.5 2.3 %collective-permute-done.2.refs_2_.refs_3_.refs_4_.refs_5_ = bf16[128,3072]{1,0:T(8,128)(2,1)S(1)} collective-permute-done((bf16[128,3072]{1,0:T(8,128)(2,1)}, bf16[128,3072]{1,0:T(8,128)(2,1)S(1)}, u32[]{:S(2)}, u32[]{:S(2)}) %collective-permute-start.2) | collective-permute-done | bytes 786464 | tf_op jit(solution)/shard_map/ppermute | solution.py:38
  24.8 1.5 regroup.6
  27.5 7.1 %project.2 = (bf16[512,128]{1,0:T(8,128)(2,1)S(1)}, bf16[512,256]{1,0:T(8,128)(2,1)S(1)}, bf16[512,384]{1,0:T(8,128)(2,1)}) custom-call(bf16[128,3072]{1,0:T(8,128)(2,1)S(1)} %copy-done.11, bf16[128,3072]{1,0:T(8,128)(2,1)S(1)} %collective-permute-done.refs_0_.refs_1_.refs_8_.refs_9_, ...), custom_call_target="tpu_custom_call" | custom-call | tf_op jit(solution)/shard_map/project/pallas_call | solution.py:110
  35.3 2.2 %collective-permute-start.4 = (bf16[512,384]{1,0:T(8,128)(2,1)}, bf16[512,384]{1,0:T(8,128)(2,1)S(1)}, u32[]{:S(2)}, u32[]{:S(2)}) collective-permute-start(bf16[512,384]{1,0:T(8,128)(2,1)} %get-tuple-element.20), channel_id=1, source_target_pairs={{0,8},{1,9},{2,10},{3,11},{4,12},{5,13},{6,14},{7,15},{8,0},{9,1},... | collective-permute-start | bytes 1179656 | tf_op jit(solution)/shard_map/ppermute | solution.py:38
  37.5 2.7 %collective-permute-start.6 = (bf16[128,3072]{1,0:T(8,128)(2,1)}, bf16[128,3072]{1,0:T(8,128)(2,1)}, u32[]{:S(2)}, u32[]{:S(2)}) collective-permute-start(bf16[128,3072]{1,0:T(8,128)(2,1)} %get-tuple-element.21), channel_id=1, source_target_pairs={{0,48},{1,49},{2,50},{3,51},{4,52},{5,53},{6,54},{7,55},{8,56},{9,... | collective-permute-start | bytes 2359304 | tf_op jit(solution)/shard_map/ppermute | solution.py:38
  40.1 2.7 %collective-permute-start.7 = (bf16[128,3072]{1,0:T(8,128)(2,1)}, bf16[128,3072]{1,0:T(8,128)(2,1)}, u32[]{:S(2)}, u32[]{:S(2)}) collective-permute-start(bf16[128,3072]{1,0:T(8,128)(2,1)} %get-tuple-element.22), channel_id=1, source_target_pairs={{0,64},{1,65},{2,66},{3,67},{4,68},{5,69},{6,70},{7,71},{8,72},{9,... | collective-permute-start | bytes 2359304 | tf_op jit(solution)/shard_map/ppermute | solution.py:38
  46.0 1.4 collective-permute-start.9
  51.0 9.5 %collective-permute-done.5.refs_4_.refs_0_ = bf16[128,3072]{1,0:T(8,128)(2,1)} collective-permute-done((bf16[128,3072]{1,0:T(8,128)(2,1)}, bf16[128,3072]{1,0:T(8,128)(2,1)}, u32[]{:S(2)}, u32[]{:S(2)}) %collective-permute-start.5) | collective-permute-done | bytes 786464 | tf_op jit(solution)/shard_map/ppermute | solution.py:38
  61.8 1.6 copy-done.2
  63.4 6.6 %project.3 = (bf16[512,128]{1,0:T(8,128)(2,1)S(1)}, bf16[512,256]{1,0:T(8,128)(2,1)S(1)}, bf16[512,384]{1,0:T(8,128)(2,1)S(1)}) custom-call(bf16[128,3072]{1,0:T(8,128)(2,1)} %collective-permute-done.5.refs_4_.refs_0_, bf16[128,3072]{1,0:T(8,128)(2,1)} %collective-permute-done.6.refs_5_.refs_1_, bf16[128,3072]{1,0:T(8,128)(2,1)} %collective-permute-done.7.refs_6_.refs_2_, ...), custom_call_target="tpu_custom_call" | custom-call | tf_op jit(solution)/shard_map/project/pallas_call | solution.py:110
  70.0 1.5 collective-permute-start.11
  71.5 1.2 collective-permute-start.12
  72.7 2.0 %collective-permute-start.14 = (bf16[1024,256]{1,0:T(8,128)(2,1)S(1)}, bf16[1024,256]{1,0:T(8,128)(2,1)S(1)}, u32[]{:S(2)}, u32[]{:S(2)}) collective-permute-start(bf16[1024,256]{1,0:T(8,128)(2,1)S(1)} %regroup.9.refs_7_), channel_id=1, source_target_pairs={{0,4},{1,5},{2,6},{3,7},{4,0},{5,1},{6,2},{7,3},{8,12},{9,13},{10,... | collective-permute-start | bytes 1572872 | tf_op jit(solution)/shard_map/ppermute | solution.py:38
  76.3 1.4 collective-permute-start.17
  77.8 1.6 collective-permute-done.12.refs_1_.refs_3_
  79.4 1.2 collective-permute-start.13
  81.1 12.9 %attention.3 = (f32[4096,256]{1,0:T(8,128)}, f32[4096,128]{1,0:T(8,128)}) custom-call(bf16[1024,128]{1,0:T(8,128)(2,1)} %copy-done.7, bf16[1024,128]{1,0:T(8,128)(2,1)} %copy-done.17, bf16[1024,256]{1,0:T(8,128)(2,1)} %copy-done.5, bf16[1024,256]{1,0:T(8,128)(2,1)} %copy-done.4, bf16[1024,256]{1,0:T(8,128)(2,1)} %copy-done.3, bf16[1024,256]{1,0:T(8,128)(2,1)} %copy-done.6), custom_call_target="tpu_custom_call" | custom-call | tf_op jit(solution)/shard_map/attention/pallas_call | solution.py:246
  94.7 12.8 %attention.4 = (f32[4096,256]{1,0:T(8,128)}, f32[4096,128]{1,0:T(8,128)}) custom-call(bf16[1024,128]{1,0:T(8,128)(2,1)} %copy-done.8, bf16[1024,128]{1,0:T(8,128)(2,1)} %copy-done.18, bf16[1024,256]{1,0:T(8,128)(2,1)} %copy-done.5, bf16[1024,256]{1,0:T(8,128)(2,1)} %copy-done.4, ...), custom_call_target="tpu_custom_call", output_to_operand_aliasing={{0}: (6, {}), {1}: (7, {})} | custom-call | tf_op jit(solution)/shard_map/attention/pallas_call | solution.py:246
  107.6 2.3 %collective-permute-done.17.refs_8_ = bf16[1024,256]{1,0:T(8,128)(2,1)S(1)} collective-permute-done((bf16[1024,256]{1,0:T(8,128)(2,1)S(1)}, bf16[1024,256]{1,0:T(8,128)(2,1)S(1)}, u32[]{:S(2)}, u32[]{:S(2)}) %collective-permute-start.17) | collective-permute-done | bytes 524320 | tf_op jit(solution)/shard_map/ppermute | solution.py:38
  110.7 25.8 %attention.5 = bf16[2,4,2,2,80,128]{5,4,3,2,1,0:T(8,128)(2,1)} custom-call(s32[4]{0:T(128)} %pad_add_fusion.1.refs_0_, bf16[1024,128]{1,0:T(8,128)(2,1)} %copy-done.7, bf16[1024,128]{1,0:T(8,128)(2,1)} %copy-done.8, bf16[1024,128]{1,0:T(8,128)(2,1)} %copy-done.17, bf16[1024,128]{1,0:T(8,128)(2,1)} %copy-done.18, bf16[1024,256]{1,0:T(8,128)(2,1)} %copy-done.19, ...), custom_call_target="tpu_custom_call" | custom-call | tf_op jit(solution)/shard_map/attention/pallas_call | solution.py:246
  136.5 18.1 %all_to_all.10.parts_ref = bf16[32,80,128]{2,1,0:T(8,128)(2,1)} all-to-all(bf16[32,80,128]{2,1,0:T(8,128)(2,1)} %bitcast.28), channel_id=1, replica_groups=mesh['xh'=2,'z'=4,'c'=2,'y'=4,'xl'=2] {'xh','z','c','xl'}, dimensions={0} | all-to-all | bytes 1310720 | tf_op jit(solution)/shard_map/all_to_all | solution.py:519
  154.5 2.3 %latent_tile.1 = bf16[64,64,128]{2,1,0:T(8,128)(2,1)} custom-call(bf16[32,80,128]{2,1,0:T(8,128)(2,1)} %all_to_all.10.parts_ref, f32[64,128]{1,0:T(8,128)} %bitcast.25), custom_call_target="tpu_custom_call" | custom-call | tf_op jit(solution)/shard_map/latent_tile/pallas_call | solution.py:283
  156.9 23.1 %all_to_all.11.own_ref = bf16[64,64,128]{2,1,0:T(8,128)(2,1)S(1)} all-to-all(bf16[64,64,128]{2,1,0:T(8,128)(2,1)} %latent_tile.1), channel_id=1, replica_groups=mesh['xh'=2,'z'=4,'c'=2,'y'=4,'xl'=2] {'xh','z','y','xl'}, dimensions={0} | all-to-all | bytes 2097152 | tf_op jit(solution)/shard_map/all_to_all | solution.py:522
  180.0 2.3 %collective-permute-start.18 = (bf16[64,64,128]{2,1,0:T(8,128)(2,1)S(1)}, bf16[64,64,128]{2,1,0:T(8,128)(2,1)S(1)}, u32[]{:S(2)}, u32[]{:S(2)}) collective-permute-start(bf16[64,64,128]{2,1,0:T(8,128)(2,1)S(1)} %all_to_all.11.own_ref), channel_id=1, source_target_pairs={{0,8},{1,9},{2,10},{3,11},{4,12},{5,13},{6,14},{7,15},{8,0},{9,1},... | collective-permute-start | bytes 3145736 | tf_op jit(solution)/shard_map/ppermute | solution.py:38
  182.3 2.3 %collective-permute-done.18.other_ref = bf16[64,64,128]{2,1,0:T(8,128)(2,1)S(1)} collective-permute-done((bf16[64,64,128]{2,1,0:T(8,128)(2,1)S(1)}, bf16[64,64,128]{2,1,0:T(8,128)(2,1)S(1)}, u32[]{:S(2)}, u32[]{:S(2)}) %collective-permute-start.18) | collective-permute-done | bytes 1048608 | tf_op jit(solution)/shard_map/ppermute | solution.py:38
  184.6 12.0 %decode.1 = bf16[1,4,512,2048]{3,2,1,0:T(8,128)(2,1)} custom-call(s32[17]{0:T(128)S(1)} %pad_add_fusion.refs_8_.ids_ref, bf16[64,64,128]{2,1,0:T(8,128)(2,1)S(1)} %all_to_all.11.own_ref, bf16[64,64,128]{2,1,0:T(8,128)(2,1)S(1)} %collective-permute-done.18.other_ref, bf16[512,512]{1,0:T(8,128)(2,1)S(1)} %copy-done.12, ...), custom_call_target="tpu_custom_call" | custom-call | tf_op jit(solution)/shard_map/decode/pallas_call | solution.py:405
  (97 shorter events, 13.4 us)
Async XLA Ops:
  0.0 48.1 %copy-start = (bf16[2048,64]{0,1:T(8,128)(2,1)S(1)}, bf16[2048,64]{0,1:T(8,128)(2,1)}, u32[]{:S(2)}) copy-start(bf16[2048,64]{0,1:T(8,128)(2,1)} %param.13) | copy-start | bytes 786436
  0.0 26.4 %collective-permute-start.3 = (bf16[3,3072,128]{2,1,0:T(8,128)(2,1)}, bf16[3,3072,128]{2,1,0:T(8,128)(2,1)}, u32[]{:S(2)}, u32[]{:S(2)}) collective-permute-start(bf16[3,3072,128]{2,1,0:T(8,128)(2,1)} %refs_4_.3), channel_id=1, source_target_pairs={{0,8},{1,9},{2,10},{3,11},{4,12},{5,13},{6,14},{7,15},{8,0},{9,1},... | collective-permute-start | bytes 7077896 | tf_op jit(solution)/shard_map/ppermute | solution.py:38
  0.7 21.8 %collective-permute-start = (bf16[128,3072]{1,0:T(8,128)(2,1)}, bf16[128,3072]{1,0:T(8,128)(2,1)S(1)}, u32[]{:S(2)}, u32[]{:S(2)}) collective-permute-start(bf16[128,3072]{1,0:T(8,128)(2,1)} %refs_0_.1), channel_id=1, source_target_pairs={{0,16},{1,17},{2,18},{3,19},{4,20},{5,21},{6,22},{7,23},{8,24},{9,... | collective-permute-start | bytes 2359304 | tf_op jit(solution)/shard_map/ppermute | solution.py:38
  2.3 20.2 %collective-permute-start.1 = (bf16[128,3072]{1,0:T(8,128)(2,1)}, bf16[128,3072]{1,0:T(8,128)(2,1)S(1)}, u32[]{:S(2)}, u32[]{:S(2)}) collective-permute-start(bf16[128,3072]{1,0:T(8,128)(2,1)} %refs_0_.1), channel_id=1, source_target_pairs={{0,48},{1,49},{2,50},{3,51},{4,52},{5,53},{6,54},{7,55},{8,56},{9,... | collective-permute-start | bytes 2359304 | tf_op jit(solution)/shard_map/ppermute | solution.py:38
  4.4 20.4 %collective-permute-start.2 = (bf16[128,3072]{1,0:T(8,128)(2,1)}, bf16[128,3072]{1,0:T(8,128)(2,1)S(1)}, u32[]{:S(2)}, u32[]{:S(2)}) collective-permute-start(bf16[128,3072]{1,0:T(8,128)(2,1)} %refs_0_.1), channel_id=1, source_target_pairs={{0,64},{1,65},{2,66},{3,67},{4,68},{5,69},{6,70},{7,71},{8,72},{9,... | collective-permute-start | bytes 2359304 | tf_op jit(solution)/shard_map/ppermute | solution.py:38
  7.2 38.9 %collective-permute-start.8 = (bf16[128,3072]{1,0:T(8,128)(2,1)}, bf16[128,3072]{1,0:T(8,128)(2,1)}, u32[]{:S(2)}, u32[]{:S(2)}) collective-permute-start(bf16[128,3072]{1,0:T(8,128)(2,1)} %refs_0_.1), channel_id=1, source_target_pairs={{0,96},{1,97},{2,98},{3,99},{4,100},{5,101},{6,102},{7,103},{8,104... | collective-permute-start | bytes 2359304 | tf_op jit(solution)/shard_map/ppermute | solution.py:38
  27.5 15.4 %copy-start.26 = (s32[128]{0:T(128)S(1)}, s32[128]{0:T(128)}, u32[]{:S(2)}) copy-start(s32[128]{0:T(128)} %param.17) | copy-start | bytes 1540
  27.5 16.8 %copy-start.23 = (s32[256,4]{0,1:T(4,128)S(1)}, s32[256,4]{0,1:T(4,128)}, u32[]{:S(2)}) copy-start(s32[256,4]{0,1:T(4,128)} %param.18) | copy-start | bytes 12292
  27.5 20.6 %copy-start.24 = (f32[512]{0:T(512)S(1)}, f32[512]{0:T(512)}, u32[]{:S(2)}) copy-start(f32[512]{0:T(512)} %param.15) | copy-start | bytes 6148
  27.5 20.8 %copy-start.25 = (f32[512]{0:T(512)S(1)}, f32[512]{0:T(512)}, u32[]{:S(2)}) copy-start(f32[512]{0:T(512)} %param.16) | copy-start | bytes 6148
  35.3 13.0 %copy-start.9 = (bf16[512,256]{1,0:T(8,128)(2,1)}, bf16[512,256]{1,0:T(8,128)(2,1)S(1)}, u32[]{:S(2)}) copy-start(bf16[512,256]{1,0:T(8,128)(2,1)S(1)} %get-tuple-element.23.refs_0_) | copy-start | bytes 786436
  35.3 10.5 %collective-permute-start.4 = (bf16[512,384]{1,0:T(8,128)(2,1)}, bf16[512,384]{1,0:T(8,128)(2,1)S(1)}, u32[]{:S(2)}, u32[]{:S(2)}) collective-permute-start(bf16[512,384]{1,0:T(8,128)(2,1)} %get-tuple-element.20), channel_id=1, source_target_pairs={{0,8},{1,9},{2,10},{3,11},{4,12},{5,13},{6,14},{7,15},{8,0},{9,1},... | collective-permute-start | bytes 1179656 | tf_op jit(solution)/shard_map/ppermute | solution.py:38
  37.5 23.0 %collective-permute-start.5 = (bf16[128,3072]{1,0:T(8,128)(2,1)}, bf16[128,3072]{1,0:T(8,128)(2,1)}, u32[]{:S(2)}, u32[]{:S(2)}) collective-permute-start(bf16[128,3072]{1,0:T(8,128)(2,1)} %get-tuple-element.18.refs_6_), channel_id=1, source_target_pairs={{0,16},{1,17},{2,18},{3,19},{4,20},{5,21},{6,22},{7,23},{8,24},{9,... | collective-permute-start | bytes 2359304 | tf_op jit(solution)/shard_map/ppermute | solution.py:38
  37.5 23.0 %collective-permute-start.6 = (bf16[128,3072]{1,0:T(8,128)(2,1)}, bf16[128,3072]{1,0:T(8,128)(2,1)}, u32[]{:S(2)}, u32[]{:S(2)}) collective-permute-start(bf16[128,3072]{1,0:T(8,128)(2,1)} %get-tuple-element.21), channel_id=1, source_target_pairs={{0,48},{1,49},{2,50},{3,51},{4,52},{5,53},{6,54},{7,55},{8,56},{9,... | collective-permute-start | bytes 2359304 | tf_op jit(solution)/shard_map/ppermute | solution.py:38
  40.1 20.4 %collective-permute-start.7 = (bf16[128,3072]{1,0:T(8,128)(2,1)}, bf16[128,3072]{1,0:T(8,128)(2,1)}, u32[]{:S(2)}, u32[]{:S(2)}) collective-permute-start(bf16[128,3072]{1,0:T(8,128)(2,1)} %get-tuple-element.22), channel_id=1, source_target_pairs={{0,64},{1,65},{2,66},{3,67},{4,68},{5,69},{6,70},{7,71},{8,72},{9,... | collective-permute-start | bytes 2359304 | tf_op jit(solution)/shard_map/ppermute | solution.py:38
  45.8 15.9 %copy-start.5 = (bf16[1024,256]{1,0:T(8,128)(2,1)}, bf16[1024,256]{1,0:T(8,128)(2,1)S(1)}, u32[]{:S(2)}) copy-start(bf16[1024,256]{1,0:T(8,128)(2,1)S(1)} %regroup.8.refs_2_) | copy-start | bytes 1572868
  45.8 14.7 %collective-permute-start.10 = (bf16[1024,256]{1,0:T(8,128)(2,1)S(1)}, bf16[1024,256]{1,0:T(8,128)(2,1)S(1)}, u32[]{:S(2)}, u32[]{:S(2)}) collective-permute-start(bf16[1024,256]{1,0:T(8,128)(2,1)S(1)} %regroup.8.refs_2_), channel_id=1, source_target_pairs={{0,6},{1,7},{2,0},{3,1},{4,2},{5,3},{6,4},{7,5},{8,14},{9,15},{10,... | collective-permute-start | bytes 1572872 | tf_op jit(solution)/shard_map/ppermute | solution.py:38
  46.0 14.5 %collective-permute-start.9 = (bf16[1024,256]{1,0:T(8,128)(2,1)S(1)}, bf16[1024,256]{1,0:T(8,128)(2,1)S(1)}, u32[]{:S(2)}, u32[]{:S(2)}) collective-permute-start(bf16[1024,256]{1,0:T(8,128)(2,1)S(1)} %regroup.8.refs_2_), channel_id=1, source_target_pairs={{0,2},{1,3},{2,4},{3,5},{4,6},{5,7},{6,0},{7,1},{8,10},{9,11},{10,... | collective-permute-start | bytes 1572872 | tf_op jit(solution)/shard_map/ppermute | solution.py:38
  48.1 13.6 %copy-start.14 = (bf16[4,16,128]{2,1,0:T(8,128)(2,1)}, bf16[4,16,128]{2,1,0:T(8,128)(2,1)S(1)}, u32[]{:S(2)}) copy-start(bf16[4,16,128]{2,1,0:T(8,128)(2,1)S(1)} %copy.20) | copy-start | bytes 49156
  49.2 12.5 %copy-start.13 = (f32[128,16,4]{0,1,2:T(8,128)}, f32[128,16,4]{0,1,2:T(8,128)S(1)}, u32[]{:S(2)}) copy-start(f32[128,16,4]{0,1,2:T(8,128)S(1)} %copy.21) | copy-start | bytes 98308
  51.0 20.5 %copy-start.7 = (bf16[1024,128]{1,0:T(8,128)(2,1)}, bf16[1024,128]{1,0:T(8,128)(2,1)S(1)}, u32[]{:S(2)}) copy-start(bf16[1024,128]{1,0:T(8,128)(2,1)S(1)} %regroup.7.refs_6_.refs_0_.refs_1_) | copy-start | bytes 786436
  70.0 4.7 %collective-permute-start.11 = (bf16[512,384]{1,0:T(8,128)(2,1)S(1)}, bf16[512,384]{1,0:T(8,128)(2,1)S(1)}, u32[]{:S(2)}, u32[]{:S(2)}) collective-permute-start(bf16[512,384]{1,0:T(8,128)(2,1)S(1)} %get-tuple-element.25), channel_id=1, source_target_pairs={{0,8},{1,9},{2,10},{3,11},{4,12},{5,13},{6,14},{7,15},{8,0},{9,1},... | collective-permute-start | bytes 1179656 | tf_op jit(solution)/shard_map/ppermute | solution.py:38
  71.5 7.9 %collective-permute-start.12 = (bf16[1024,128]{1,0:T(8,128)(2,1)S(1)}, bf16[1024,128]{1,0:T(8,128)(2,1)S(1)}, u32[]{:S(2)}, u32[]{:S(2)}) collective-permute-start(bf16[1024,128]{1,0:T(8,128)(2,1)S(1)} %regroup.7.refs_6_.refs_0_.refs_1_), channel_id=1, source_target_pairs={{0,1},{1,0},{2,3},{3,2},{4,5},{5,4},{6,7},{7,6},{8,9},{9,8},{10,11... | collective-permute-start | bytes 786440 | tf_op jit(solution)/shard_map/ppermute | solution.py:38
  72.7 34.8 %collective-permute-start.14 = (bf16[1024,256]{1,0:T(8,128)(2,1)S(1)}, bf16[1024,256]{1,0:T(8,128)(2,1)S(1)}, u32[]{:S(2)}, u32[]{:S(2)}) collective-permute-start(bf16[1024,256]{1,0:T(8,128)(2,1)S(1)} %regroup.9.refs_7_), channel_id=1, source_target_pairs={{0,4},{1,5},{2,6},{3,7},{4,0},{5,1},{6,2},{7,3},{8,12},{9,13},{10,... | collective-permute-start | bytes 1572872 | tf_op jit(solution)/shard_map/ppermute | solution.py:38
  74.8 6.4 %copy-start.6 = (bf16[1024,256]{1,0:T(8,128)(2,1)}, bf16[1024,256]{1,0:T(8,128)(2,1)S(1)}, u32[]{:S(2)}) copy-start(bf16[1024,256]{1,0:T(8,128)(2,1)S(1)} %regroup.11.refs_5_) | copy-start | bytes 1572868
  74.8 32.8 %collective-permute-start.15 = (bf16[1024,256]{1,0:T(8,128)(2,1)S(1)}, bf16[1024,256]{1,0:T(8,128)(2,1)S(1)}, u32[]{:S(2)}, u32[]{:S(2)}) collective-permute-start(bf16[1024,256]{1,0:T(8,128)(2,1)S(1)} %regroup.11.refs_5_), channel_id=1, source_target_pairs={{0,2},{1,3},{2,4},{3,5},{4,6},{5,7},{6,0},{7,1},{8,10},{9,11},{10,... | collective-permute-start | bytes 1572872 | tf_op jit(solution)/shard_map/ppermute | solution.py:38
  75.5 32.1 %collective-permute-start.16 = (bf16[1024,256]{1,0:T(8,128)(2,1)S(1)}, bf16[1024,256]{1,0:T(8,128)(2,1)S(1)}, u32[]{:S(2)}, u32[]{:S(2)}) collective-permute-start(bf16[1024,256]{1,0:T(8,128)(2,1)S(1)} %regroup.11.refs_5_), channel_id=1, source_target_pairs={{0,6},{1,7},{2,0},{3,1},{4,2},{5,3},{6,4},{7,5},{8,14},{9,15},{10,... | collective-permute-start | bytes 1572872 | tf_op jit(solution)/shard_map/ppermute | solution.py:38
  76.3 33.6 %collective-permute-start.17 = (bf16[1024,256]{1,0:T(8,128)(2,1)S(1)}, bf16[1024,256]{1,0:T(8,128)(2,1)S(1)}, u32[]{:S(2)}, u32[]{:S(2)}) collective-permute-start(bf16[1024,256]{1,0:T(8,128)(2,1)S(1)} %regroup.11.refs_5_), channel_id=1, source_target_pairs={{0,4},{1,5},{2,6},{3,7},{4,0},{5,1},{6,2},{7,3},{8,12},{9,13},{10,... | collective-permute-start | bytes 1572872 | tf_op jit(solution)/shard_map/ppermute | solution.py:38
  77.8 16.3 %copy-start.8 = (bf16[1024,128]{1,0:T(8,128)(2,1)}, bf16[1024,128]{1,0:T(8,128)(2,1)S(1)}, u32[]{:S(2)}) copy-start(bf16[1024,128]{1,0:T(8,128)(2,1)S(1)} %regroup.10.refs_0_.refs_2_) | copy-start | bytes 786436
  79.4 14.6 %collective-permute-start.13 = (bf16[1024,128]{1,0:T(8,128)(2,1)S(1)}, bf16[1024,128]{1,0:T(8,128)(2,1)S(1)}, u32[]{:S(2)}, u32[]{:S(2)}) collective-permute-start(bf16[1024,128]{1,0:T(8,128)(2,1)S(1)} %regroup.10.refs_0_.refs_2_), channel_id=1, source_target_pairs={{0,1},{1,0},{2,3},{3,2},{4,5},{5,4},{6,7},{7,6},{8,9},{9,8},{10,11... | collective-permute-start | bytes 786440 | tf_op jit(solution)/shard_map/ppermute | solution.py:38
  136.4 48.2 %copy-start.12 = (bf16[512,512]{1,0:T(8,128)(2,1)S(1)}, bf16[512,512]{1,0:T(8,128)(2,1)}, u32[]{:S(2)}) copy-start(bf16[512,512]{1,0:T(8,128)(2,1)} %constant.90.clone.place_ref) | copy-start | bytes 1572868
  180.0 4.6 %collective-permute-start.18 = (bf16[64,64,128]{2,1,0:T(8,128)(2,1)S(1)}, bf16[64,64,128]{2,1,0:T(8,128)(2,1)S(1)}, u32[]{:S(2)}, u32[]{:S(2)}) collective-permute-start(bf16[64,64,128]{2,1,0:T(8,128)(2,1)S(1)} %all_to_all.11.own_ref), channel_id=1, source_target_pairs={{0,8},{1,9},{2,10},{3,11},{4,12},{5,13},{6,14},{7,15},{8,0},{9,1},... | collective-permute-start | bytes 3145736 | tf_op jit(solution)/shard_map/ppermute | solution.py:38
  (14 other events, 22.4 us)
where the time goes:
time: 199 us; the launch traced here: 197 us
  Pallas kernels  81.3 us (41%)
  blocking collectives  41.2 us (21%)
  waiting for transfers between devices  30.1 us (15%)
  starting transfers between devices  28.8 us (14%)
  local copies, waits for them, and re-layouts  11.4 us (6%)
  other arithmetic  2.12 us (1%)
    pallas_call x3, Pallas kernels, attention(): pl.pallas_call(functools.partial(attention_kernel, bk, len(qs), len(kvs),...  51.5 us
    ppermute x19, waiting for transfers between devices, shift(): return lax.ppermute(x, AXES, pairs)  30.1 us
    ppermute x19, starting transfers between devices, shift(): return lax.ppermute(x, AXES, pairs)  28.8 us
    all_to_all x1, blocking collectives, body(): lax.all_to_all(tile, ('xh', 'z', 'y', 'xl'), split_axis=0, concat_axis=0,...  23.1 us
    all_to_all x1, blocking collectives, body(): lax.all_to_all(parts, SEQ + ('xl',), split_axis=0, concat_axis=0, tiled=T...  18.1 us
    pallas_call x2, Pallas kernels, project(): pl.pallas_call(functools.partial(project_kernel, q_order, scale, len(afte...  13.8 us
    pallas_call x1, Pallas kernels, decode(): pl.pallas_call(decode_kernel, grid_spec=pltpu.PrefetchScalarGridSpec(num_...  12 us
    unnamed x56, local copies, waits for them, and re-layouts  8.31 us
  transfers between devices with their start and end apart: 19, of which 6 were waited for; matrix products, arithmetic and copies ran while one was open for 3% of the time, Pallas kernels for 18%

commit v1 on v0

--- a/solution.py
+++ b/solution.py
@@ -122,21 +122,18 @@
     )(*xs, own_weight, other_weight, *after)
 
 
-def softmax_blocks(q, kv_refs, value_ref, bk, run_max, acc):
-    places, start = [], 0
-    for ref in kv_refs:
-        for i in range(0, ref.shape[0], bk):
-            places.append((ref, i, start + i))
-        start += ref.shape[0]
+def softmax_blocks(q, kv_refs, bk, run_max, acc):
+    places = [(ref, i) for ref in kv_refs for i in range(0, ref.shape[0], bk)]
+    ones = jnp.ones((bk, HEAD_DIM), jnp.bfloat16)
 
     def scores_of(n):
-        ref, i, _ = places[n]
+        ref, i = places[n]
         return lax.dot_general(
             q, ref[i : i + bk, :HEAD_DIM], NT, preferred_element_type=jnp.float32
         )
 
     following = scores_of(0)
-    for n, (_, _, row) in enumerate(places):
+    for n, (ref, i) in enumerate(places):
         scores = following
         if n + 1 < len(places):
             following = scores_of(n + 1)
@@ -144,7 +141,8 @@
         if run_max is not None:
             new_max = jnp.maximum(run_max, new_max)
         probs = jnp.exp2(scores - new_max).astype(jnp.bfloat16)
-        part = jnp.dot(probs, value_ref[row : row + bk, :], preferred_element_type=jnp.float32)
+        values = jnp.concatenate([ref[i : i + bk, HEAD_DIM:], ones], axis=1)
+        part = jnp.dot(probs, values, preferred_element_type=jnp.float32)
         acc = part if acc is None else acc * jnp.exp2(run_max - new_max) + part
         run_max = new_max
     return run_max, acc
@@ -159,18 +157,9 @@
         acc_in_ref, max_in_ref, *refs = refs
     refs = refs[n_into:]
     if final:
-        w_ref, out_ref, value_ref = refs
+        w_ref, out_ref = refs
     else:
-        acc_out_ref, max_out_ref, value_ref = refs
-
-    @pl.when(pl.program_id(0) == 0)
-    def _():
-        start = 0
-        for ref in kv_refs:
-            n = ref.shape[0]
-            value_ref[start : start + n, :HEAD_DIM] = ref[:, HEAD_DIM:]
-            value_ref[start : start + n, HEAD_DIM:] = jnp.ones((n, HEAD_DIM), jnp.bfloat16)
-            start += n
+        acc_out_ref, max_out_ref = refs
 
     q = q_refs[0][...]
     for n in range(1, n_q):
@@ -179,7 +168,7 @@
     run_max, acc = None, None
     if carry_in:
         run_max, acc = jnp.max(max_in_ref[...], axis=1, keepdims=True), acc_in_ref[...]
-    run_max, acc = softmax_blocks(q, kv_refs, value_ref, bk, run_max, acc)
+    run_max, acc = softmax_blocks(q, kv_refs, bk, run_max, acc)
     if not final:
         acc_out_ref[...] = acc
         max_out_ref[...] = jnp.broadcast_to(run_max, max_out_ref.shape)
@@ -215,7 +204,6 @@
 
 def attention(qs, kvs, carry=None, fresh=False, blocks=(1, 0), last=None, bk=512):
     bq = qs[0].shape[0]
-    length = sum(kv.shape[0] for kv in kvs)
     stride, offset = blocks
     widths = (2 * HEAD_DIM, HEAD_DIM)
     whole = lambda x: pl.BlockSpec(x.shape, lambda i, *p: (0, 0))
@@ -252,7 +240,6 @@
             grid=(len(qs),),
             in_specs=in_specs,
             out_specs=out_specs,
-            scratch_shapes=[pltpu.VMEM((length, 2 * HEAD_DIM), jnp.bfloat16)],
         ),
         out_shape=out_shape,
         input_output_aliases=aliases,

time: 199 us -> 200 us (level)
  transfers between devices with their start and end apart: 19 -> 19, of which waited for: 6 -> 6; matrix products, arithmetic and copies ran while one was open for 3% -> 3% of each run, Pallas kernels for 18% -> 17%
where the time goes in v1:
time: 200 us; the launch traced here: 198 us
  Pallas kernels  82.2 us (41%)
  blocking collectives  41.2 us (21%)
  waiting for transfers between devices  30.8 us (15%)
  starting transfers between devices  28.8 us (14%)
  local copies, waits for them, and re-layouts  11.4 us (6%)
  other arithmetic  2.12 us (1%)
    pallas_call x3, Pallas kernels, attention(): pl.pallas_call(functools.partial(attention_kernel, bk, len(qs), len(kvs),...  50.4 us
    ppermute x19, waiting for transfers between devices, shift(): return lax.ppermute(x, AXES, pairs)  30.8 us
    ppermute x19, starting transfers between devices, shift(): return lax.ppermute(x, AXES, pairs)  28.8 us
    all_to_all x1, blocking collectives, body(): lax.all_to_all(tile, ('xh', 'z', 'y', 'xl'), split_axis=0, concat_axis=0,...  23.1 us
    all_to_all x1, blocking collectives, body(): lax.all_to_all(parts, SEQ + ('xl',), split_axis=0, concat_axis=0, tiled=T...  18.1 us
    pallas_call x1, Pallas kernels, decode(): pl.pallas_call(decode_kernel, grid_spec=pltpu.PrefetchScalarGridSpec(num_...  14 us
    pallas_call x2, Pallas kernels, project(): pl.pallas_call(functools.partial(project_kernel, q_order, scale, len(afte...  13.8 us
    unnamed x56, local copies, waits for them, and re-layouts  8.31 us
  transfers between devices with their start and end apart: 19, of which 6 were waited for; matrix products, arithmetic and copies ran while one was open for 3% of the time, Pallas kernels for 17%

profile of v1, /device:TPU:9, one launch (start us, length us, event | category | flops | bytes accessed | tf_op | source)
XLA Modules:
  0.0 198.2 jit_solution(18266004503108373150)
XLA Ops:
  0.7 1.6 collective-permute-start
  2.3 2.1 %collective-permute-start.1 = (bf16[128,3072]{1,0:T(8,128)(2,1)}, bf16[128,3072]{1,0:T(8,128)(2,1)S(1)}, u32[]{:S(2)}, u32[]{:S(2)}) collective-permute-start(bf16[128,3072]{1,0:T(8,128)(2,1)} %refs_0_.1), channel_id=1, source_target_pairs={{0,48},{1,49},{2,50},{3,51},{4,52},{5,53},{6,54},{7,55},{8,56},{9,... | collective-permute-start | bytes 2359304 | tf_op jit(solution)/shard_map/ppermute | solution.py:38
  4.4 2.7 %collective-permute-start.2 = (bf16[128,3072]{1,0:T(8,128)(2,1)}, bf16[128,3072]{1,0:T(8,128)(2,1)S(1)}, u32[]{:S(2)}, u32[]{:S(2)}) collective-permute-start(bf16[128,3072]{1,0:T(8,128)(2,1)} %refs_0_.1), channel_id=1, source_target_pairs={{0,64},{1,65},{2,66},{3,67},{4,68},{5,69},{6,70},{7,71},{8,72},{9,... | collective-permute-start | bytes 2359304 | tf_op jit(solution)/shard_map/ppermute | solution.py:38
  7.2 1.2 collective-permute-start.8
  8.4 1.2 copy.19
  10.4 12.0 %collective-permute-done.refs_0_.refs_1_.refs_8_.refs_9_ = bf16[128,3072]{1,0:T(8,128)(2,1)S(1)} collective-permute-done((bf16[128,3072]{1,0:T(8,128)(2,1)}, bf16[128,3072]{1,0:T(8,128)(2,1)S(1)}, u32[]{:S(2)}, u32[]{:S(2)}) %collective-permute-start) | collective-permute-done | bytes 786464 | tf_op jit(solution)/shard_map/ppermute | solution.py:38
  22.5 2.3 %collective-permute-done.2.refs_2_.refs_3_.refs_4_.refs_5_ = bf16[128,3072]{1,0:T(8,128)(2,1)S(1)} collective-permute-done((bf16[128,3072]{1,0:T(8,128)(2,1)}, bf16[128,3072]{1,0:T(8,128)(2,1)S(1)}, u32[]{:S(2)}, u32[]{:S(2)}) %collective-permute-start.2) | collective-permute-done | bytes 786464 | tf_op jit(solution)/shard_map/ppermute | solution.py:38
  24.8 1.5 regroup.6
  27.5 7.1 %project.2 = (bf16[512,128]{1,0:T(8,128)(2,1)S(1)}, bf16[512,256]{1,0:T(8,128)(2,1)S(1)}, bf16[512,384]{1,0:T(8,128)(2,1)}) custom-call(bf16[128,3072]{1,0:T(8,128)(2,1)S(1)} %copy-done.11, bf16[128,3072]{1,0:T(8,128)(2,1)S(1)} %collective-permute-done.refs_0_.refs_1_.refs_8_.refs_9_, ...), custom_call_target="tpu_custom_call" | custom-call | tf_op jit(solution)/shard_map/project/pallas_call | solution.py:110
  35.3 2.2 %collective-permute-start.4 = (bf16[512,384]{1,0:T(8,128)(2,1)}, bf16[512,384]{1,0:T(8,128)(2,1)S(1)}, u32[]{:S(2)}, u32[]{:S(2)}) collective-permute-start(bf16[512,384]{1,0:T(8,128)(2,1)} %get-tuple-element.20), channel_id=1, source_target_pairs={{0,8},{1,9},{2,10},{3,11},{4,12},{5,13},{6,14},{7,15},{8,0},{9,1},... | collective-permute-start | bytes 1179656 | tf_op jit(solution)/shard_map/ppermute | solution.py:38
  37.5 2.7 %collective-permute-start.6 = (bf16[128,3072]{1,0:T(8,128)(2,1)}, bf16[128,3072]{1,0:T(8,128)(2,1)}, u32[]{:S(2)}, u32[]{:S(2)}) collective-permute-start(bf16[128,3072]{1,0:T(8,128)(2,1)} %get-tuple-element.21), channel_id=1, source_target_pairs={{0,48},{1,49},{2,50},{3,51},{4,52},{5,53},{6,54},{7,55},{8,56},{9,... | collective-permute-start | bytes 2359304 | tf_op jit(solution)/shard_map/ppermute | solution.py:38
  40.1 2.7 %collective-permute-start.7 = (bf16[128,3072]{1,0:T(8,128)(2,1)}, bf16[128,3072]{1,0:T(8,128)(2,1)}, u32[]{:S(2)}, u32[]{:S(2)}) collective-permute-start(bf16[128,3072]{1,0:T(8,128)(2,1)} %get-tuple-element.22), channel_id=1, source_target_pairs={{0,64},{1,65},{2,66},{3,67},{4,68},{5,69},{6,70},{7,71},{8,72},{9,... | collective-permute-start | bytes 2359304 | tf_op jit(solution)/shard_map/ppermute | solution.py:38
  46.0 1.4 collective-permute-start.9
  51.0 9.5 %collective-permute-done.5.refs_4_.refs_0_ = bf16[128,3072]{1,0:T(8,128)(2,1)} collective-permute-done((bf16[128,3072]{1,0:T(8,128)(2,1)}, bf16[128,3072]{1,0:T(8,128)(2,1)}, u32[]{:S(2)}, u32[]{:S(2)}) %collective-permute-start.5) | collective-permute-done | bytes 786464 | tf_op jit(solution)/shard_map/ppermute | solution.py:38
  61.8 1.6 copy-done.2
  63.4 6.6 %project.3 = (bf16[512,128]{1,0:T(8,128)(2,1)S(1)}, bf16[512,256]{1,0:T(8,128)(2,1)S(1)}, bf16[512,384]{1,0:T(8,128)(2,1)S(1)}) custom-call(bf16[128,3072]{1,0:T(8,128)(2,1)} %collective-permute-done.5.refs_4_.refs_0_, bf16[128,3072]{1,0:T(8,128)(2,1)} %collective-permute-done.6.refs_5_.refs_1_, bf16[128,3072]{1,0:T(8,128)(2,1)} %collective-permute-done.7.refs_6_.refs_2_, ...), custom_call_target="tpu_custom_call" | custom-call | tf_op jit(solution)/shard_map/project/pallas_call | solution.py:110
  70.0 1.5 collective-permute-start.11
  71.5 1.2 collective-permute-start.12
  72.7 2.0 %collective-permute-start.14 = (bf16[1024,256]{1,0:T(8,128)(2,1)S(1)}, bf16[1024,256]{1,0:T(8,128)(2,1)S(1)}, u32[]{:S(2)}, u32[]{:S(2)}) collective-permute-start(bf16[1024,256]{1,0:T(8,128)(2,1)S(1)} %regroup.9.refs_7_), channel_id=1, source_target_pairs={{0,4},{1,5},{2,6},{3,7},{4,0},{5,1},{6,2},{7,3},{8,12},{9,13},{10,... | collective-permute-start | bytes 1572872 | tf_op jit(solution)/shard_map/ppermute | solution.py:38
  76.3 1.4 collective-permute-start.17
  77.8 1.6 collective-permute-done.12.refs_1_.refs_3_
  79.4 1.2 collective-permute-start.13
  81.1 12.5 %attention.3 = (f32[4096,256]{1,0:T(8,128)}, f32[4096,128]{1,0:T(8,128)}) custom-call(bf16[1024,128]{1,0:T(8,128)(2,1)} %copy-done.7, bf16[1024,128]{1,0:T(8,128)(2,1)} %copy-done.17, bf16[1024,256]{1,0:T(8,128)(2,1)} %copy-done.5, bf16[1024,256]{1,0:T(8,128)(2,1)} %copy-done.4, bf16[1024,256]{1,0:T(8,128)(2,1)} %copy-done.3, bf16[1024,256]{1,0:T(8,128)(2,1)} %copy-done.6), custom_call_target="tpu_custom_call" | custom-call | tf_op jit(solution)/shard_map/attention/pallas_call | solution.py:234
  94.4 12.5 %attention.4 = (f32[4096,256]{1,0:T(8,128)}, f32[4096,128]{1,0:T(8,128)}) custom-call(bf16[1024,128]{1,0:T(8,128)(2,1)} %copy-done.8, bf16[1024,128]{1,0:T(8,128)(2,1)} %copy-done.18, bf16[1024,256]{1,0:T(8,128)(2,1)} %copy-done.5, bf16[1024,256]{1,0:T(8,128)(2,1)} %copy-done.4, ...), custom_call_target="tpu_custom_call", output_to_operand_aliasing={{0}: (6, {}), {1}: (7, {})} | custom-call | tf_op jit(solution)/shard_map/attention/pallas_call | solution.py:234
  106.9 3.0 %collective-permute-done.17.refs_8_ = bf16[1024,256]{1,0:T(8,128)(2,1)S(1)} collective-permute-done((bf16[1024,256]{1,0:T(8,128)(2,1)S(1)}, bf16[1024,256]{1,0:T(8,128)(2,1)S(1)}, u32[]{:S(2)}, u32[]{:S(2)}) %collective-permute-start.17) | collective-permute-done | bytes 524320 | tf_op jit(solution)/shard_map/ppermute | solution.py:38
  110.7 25.3 %attention.5 = bf16[2,4,2,2,80,128]{5,4,3,2,1,0:T(8,128)(2,1)} custom-call(s32[4]{0:T(128)} %pad_add_fusion.1.refs_0_, bf16[1024,128]{1,0:T(8,128)(2,1)} %copy-done.7, bf16[1024,128]{1,0:T(8,128)(2,1)} %copy-done.8, bf16[1024,128]{1,0:T(8,128)(2,1)} %copy-done.17, bf16[1024,128]{1,0:T(8,128)(2,1)} %copy-done.18, bf16[1024,256]{1,0:T(8,128)(2,1)} %copy-done.19, ...), custom_call_target="tpu_custom_call" | custom-call | tf_op jit(solution)/shard_map/attention/pallas_call | solution.py:234
  136.0 18.1 %all_to_all.10.parts_ref = bf16[32,80,128]{2,1,0:T(8,128)(2,1)} all-to-all(bf16[32,80,128]{2,1,0:T(8,128)(2,1)} %bitcast.28), channel_id=1, replica_groups=mesh['xh'=2,'z'=4,'c'=2,'y'=4,'xl'=2] {'xh','z','c','xl'}, dimensions={0} | all-to-all | bytes 1310720 | tf_op jit(solution)/shard_map/all_to_all | solution.py:506
  154.1 2.3 %latent_tile.1 = bf16[64,64,128]{2,1,0:T(8,128)(2,1)} custom-call(bf16[32,80,128]{2,1,0:T(8,128)(2,1)} %all_to_all.10.parts_ref, f32[64,128]{1,0:T(8,128)} %bitcast.25), custom_call_target="tpu_custom_call" | custom-call | tf_op jit(solution)/shard_map/latent_tile/pallas_call | solution.py:270
  156.4 23.1 %all_to_all.11.own_ref = bf16[64,64,128]{2,1,0:T(8,128)(2,1)S(1)} all-to-all(bf16[64,64,128]{2,1,0:T(8,128)(2,1)} %latent_tile.1), channel_id=1, replica_groups=mesh['xh'=2,'z'=4,'c'=2,'y'=4,'xl'=2] {'xh','z','y','xl'}, dimensions={0} | all-to-all | bytes 2097152 | tf_op jit(solution)/shard_map/all_to_all | solution.py:509
  179.6 2.3 %collective-permute-start.18 = (bf16[64,64,128]{2,1,0:T(8,128)(2,1)S(1)}, bf16[64,64,128]{2,1,0:T(8,128)(2,1)S(1)}, u32[]{:S(2)}, u32[]{:S(2)}) collective-permute-start(bf16[64,64,128]{2,1,0:T(8,128)(2,1)S(1)} %all_to_all.11.own_ref), channel_id=1, source_target_pairs={{0,8},{1,9},{2,10},{3,11},{4,12},{5,13},{6,14},{7,15},{8,0},{9,1},... | collective-permute-start | bytes 3145736 | tf_op jit(solution)/shard_map/ppermute | solution.py:38
  181.9 2.3 %collective-permute-done.18.other_ref = bf16[64,64,128]{2,1,0:T(8,128)(2,1)S(1)} collective-permute-done((bf16[64,64,128]{2,1,0:T(8,128)(2,1)S(1)}, bf16[64,64,128]{2,1,0:T(8,128)(2,1)S(1)}, u32[]{:S(2)}, u32[]{:S(2)}) %collective-permute-start.18) | collective-permute-done | bytes 1048608 | tf_op jit(solution)/shard_map/ppermute | solution.py:38
  184.2 14.0 %decode.1 = bf16[1,4,512,2048]{3,2,1,0:T(8,128)(2,1)} custom-call(s32[17]{0:T(128)S(1)} %pad_add_fusion.refs_8_.ids_ref, bf16[64,64,128]{2,1,0:T(8,128)(2,1)S(1)} %all_to_all.11.own_ref, bf16[64,64,128]{2,1,0:T(8,128)(2,1)S(1)} %collective-permute-done.18.other_ref, bf16[512,512]{1,0:T(8,128)(2,1)S(1)} %copy-done.12, ...), custom_call_target="tpu_custom_call" | custom-call | tf_op jit(solution)/shard_map/decode/pallas_call | solution.py:392
  (97 shorter events, 13.4 us)
Async XLA Ops:
  0.0 48.1 %copy-start = (bf16[2048,64]{0,1:T(8,128)(2,1)S(1)}, bf16[2048,64]{0,1:T(8,128)(2,1)}, u32[]{:S(2)}) copy-start(bf16[2048,64]{0,1:T(8,128)(2,1)} %param.13) | copy-start | bytes 786436
  0.0 26.4 %collective-permute-start.3 = (bf16[3,3072,128]{2,1,0:T(8,128)(2,1)}, bf16[3,3072,128]{2,1,0:T(8,128)(2,1)}, u32[]{:S(2)}, u32[]{:S(2)}) collective-permute-start(bf16[3,3072,128]{2,1,0:T(8,128)(2,1)} %refs_4_.3), channel_id=1, source_target_pairs={{0,8},{1,9},{2,10},{3,11},{4,12},{5,13},{6,14},{7,15},{8,0},{9,1},... | collective-permute-start | bytes 7077896 | tf_op jit(solution)/shard_map/ppermute | solution.py:38
  0.7 21.8 %collective-permute-start = (bf16[128,3072]{1,0:T(8,128)(2,1)}, bf16[128,3072]{1,0:T(8,128)(2,1)S(1)}, u32[]{:S(2)}, u32[]{:S(2)}) collective-permute-start(bf16[128,3072]{1,0:T(8,128)(2,1)} %refs_0_.1), channel_id=1, source_target_pairs={{0,16},{1,17},{2,18},{3,19},{4,20},{5,21},{6,22},{7,23},{8,24},{9,... | collective-permute-start | bytes 2359304 | tf_op jit(solution)/shard_map/ppermute | solution.py:38
  2.3 20.2 %collective-permute-start.1 = (bf16[128,3072]{1,0:T(8,128)(2,1)}, bf16[128,3072]{1,0:T(8,128)(2,1)S(1)}, u32[]{:S(2)}, u32[]{:S(2)}) collective-permute-start(bf16[128,3072]{1,0:T(8,128)(2,1)} %refs_0_.1), channel_id=1, source_target_pairs={{0,48},{1,49},{2,50},{3,51},{4,52},{5,53},{6,54},{7,55},{8,56},{9,... | collective-permute-start | bytes 2359304 | tf_op jit(solution)/shard_map/ppermute | solution.py:38
  4.4 20.4 %collective-permute-start.2 = (bf16[128,3072]{1,0:T(8,128)(2,1)}, bf16[128,3072]{1,0:T(8,128)(2,1)S(1)}, u32[]{:S(2)}, u32[]{:S(2)}) collective-permute-start(bf16[128,3072]{1,0:T(8,128)(2,1)} %refs_0_.1), channel_id=1, source_target_pairs={{0,64},{1,65},{2,66},{3,67},{4,68},{5,69},{6,70},{7,71},{8,72},{9,... | collective-permute-start | bytes 2359304 | tf_op jit(solution)/shard_map/ppermute | solution.py:38
  7.2 38.9 %collective-permute-start.8 = (bf16[128,3072]{1,0:T(8,128)(2,1)}, bf16[128,3072]{1,0:T(8,128)(2,1)}, u32[]{:S(2)}, u32[]{:S(2)}) collective-permute-start(bf16[128,3072]{1,0:T(8,128)(2,1)} %refs_0_.1), channel_id=1, source_target_pairs={{0,96},{1,97},{2,98},{3,99},{4,100},{5,101},{6,102},{7,103},{8,104... | collective-permute-start | bytes 2359304 | tf_op jit(solution)/shard_map/ppermute | solution.py:38
  27.5 15.4 %copy-start.26 = (s32[128]{0:T(128)S(1)}, s32[128]{0:T(128)}, u32[]{:S(2)}) copy-start(s32[128]{0:T(128)} %param.17) | copy-start | bytes 1540
  27.5 16.8 %copy-start.23 = (s32[256,4]{0,1:T(4,128)S(1)}, s32[256,4]{0,1:T(4,128)}, u32[]{:S(2)}) copy-start(s32[256,4]{0,1:T(4,128)} %param.18) | copy-start | bytes 12292
  27.5 20.6 %copy-start.24 = (f32[512]{0:T(512)S(1)}, f32[512]{0:T(512)}, u32[]{:S(2)}) copy-start(f32[512]{0:T(512)} %param.15) | copy-start | bytes 6148
  27.5 20.8 %copy-start.25 = (f32[512]{0:T(512)S(1)}, f32[512]{0:T(512)}, u32[]{:S(2)}) copy-start(f32[512]{0:T(512)} %param.16) | copy-start | bytes 6148
  35.3 13.0 %copy-start.9 = (bf16[512,256]{1,0:T(8,128)(2,1)}, bf16[512,256]{1,0:T(8,128)(2,1)S(1)}, u32[]{:S(2)}) copy-start(bf16[512,256]{1,0:T(8,128)(2,1)S(1)} %get-tuple-element.23.refs_0_) | copy-start | bytes 786436
  35.3 10.5 %collective-permute-start.4 = (bf16[512,384]{1,0:T(8,128)(2,1)}, bf16[512,384]{1,0:T(8,128)(2,1)S(1)}, u32[]{:S(2)}, u32[]{:S(2)}) collective-permute-start(bf16[512,384]{1,0:T(8,128)(2,1)} %get-tuple-element.20), channel_id=1, source_target_pairs={{0,8},{1,9},{2,10},{3,11},{4,12},{5,13},{6,14},{7,15},{8,0},{9,1},... | collective-permute-start | bytes 1179656 | tf_op jit(solution)/shard_map/ppermute | solution.py:38
  37.5 23.0 %collective-permute-start.5 = (bf16[128,3072]{1,0:T(8,128)(2,1)}, bf16[128,3072]{1,0:T(8,128)(2,1)}, u32[]{:S(2)}, u32[]{:S(2)}) collective-permute-start(bf16[128,3072]{1,0:T(8,128)(2,1)} %get-tuple-element.18.refs_6_), channel_id=1, source_target_pairs={{0,16},{1,17},{2,18},{3,19},{4,20},{5,21},{6,22},{7,23},{8,24},{9,... | collective-permute-start | bytes 2359304 | tf_op jit(solution)/shard_map/ppermute | solution.py:38
  37.5 23.0 %collective-permute-start.6 = (bf16[128,3072]{1,0:T(8,128)(2,1)}, bf16[128,3072]{1,0:T(8,128)(2,1)}, u32[]{:S(2)}, u32[]{:S(2)}) collective-permute-start(bf16[128,3072]{1,0:T(8,128)(2,1)} %get-tuple-element.21), channel_id=1, source_target_pairs={{0,48},{1,49},{2,50},{3,51},{4,52},{5,53},{6,54},{7,55},{8,56},{9,... | collective-permute-start | bytes 2359304 | tf_op jit(solution)/shard_map/ppermute | solution.py:38
  40.1 20.4 %collective-permute-start.7 = (bf16[128,3072]{1,0:T(8,128)(2,1)}, bf16[128,3072]{1,0:T(8,128)(2,1)}, u32[]{:S(2)}, u32[]{:S(2)}) collective-permute-start(bf16[128,3072]{1,0:T(8,128)(2,1)} %get-tuple-element.22), channel_id=1, source_target_pairs={{0,64},{1,65},{2,66},{3,67},{4,68},{5,69},{6,70},{7,71},{8,72},{9,... | collective-permute-start | bytes 2359304 | tf_op jit(solution)/shard_map/ppermute | solution.py:38
  45.8 15.9 %copy-start.5 = (bf16[1024,256]{1,0:T(8,128)(2,1)}, bf16[1024,256]{1,0:T(8,128)(2,1)S(1)}, u32[]{:S(2)}) copy-start(bf16[1024,256]{1,0:T(8,128)(2,1)S(1)} %regroup.8.refs_2_) | copy-start | bytes 1572868
  45.8 14.7 %collective-permute-start.10 = (bf16[1024,256]{1,0:T(8,128)(2,1)S(1)}, bf16[1024,256]{1,0:T(8,128)(2,1)S(1)}, u32[]{:S(2)}, u32[]{:S(2)}) collective-permute-start(bf16[1024,256]{1,0:T(8,128)(2,1)S(1)} %regroup.8.refs_2_), channel_id=1, source_target_pairs={{0,6},{1,7},{2,0},{3,1},{4,2},{5,3},{6,4},{7,5},{8,14},{9,15},{10,... | collective-permute-start | bytes 1572872 | tf_op jit(solution)/shard_map/ppermute | solution.py:38
  46.0 14.5 %collective-permute-start.9 = (bf16[1024,256]{1,0:T(8,128)(2,1)S(1)}, bf16[1024,256]{1,0:T(8,128)(2,1)S(1)}, u32[]{:S(2)}, u32[]{:S(2)}) collective-permute-start(bf16[1024,256]{1,0:T(8,128)(2,1)S(1)} %regroup.8.refs_2_), channel_id=1, source_target_pairs={{0,2},{1,3},{2,4},{3,5},{4,6},{5,7},{6,0},{7,1},{8,10},{9,11},{10,... | collective-permute-start | bytes 1572872 | tf_op jit(solution)/shard_map/ppermute | solution.py:38
  48.1 13.6 %copy-start.14 = (bf16[4,16,128]{2,1,0:T(8,128)(2,1)}, bf16[4,16,128]{2,1,0:T(8,128)(2,1)S(1)}, u32[]{:S(2)}) copy-start(bf16[4,16,128]{2,1,0:T(8,128)(2,1)S(1)} %copy.20) | copy-start | bytes 49156
  49.2 12.5 %copy-start.13 = (f32[128,16,4]{0,1,2:T(8,128)}, f32[128,16,4]{0,1,2:T(8,128)S(1)}, u32[]{:S(2)}) copy-start(f32[128,16,4]{0,1,2:T(8,128)S(1)} %copy.21) | copy-start | bytes 98308
  51.0 20.5 %copy-start.7 = (bf16[1024,128]{1,0:T(8,128)(2,1)}, bf16[1024,128]{1,0:T(8,128)(2,1)S(1)}, u32[]{:S(2)}) copy-start(bf16[1024,128]{1,0:T(8,128)(2,1)S(1)} %regroup.7.refs_6_.refs_0_.refs_1_) | copy-start | bytes 786436
  70.0 4.7 %collective-permute-start.11 = (bf16[512,384]{1,0:T(8,128)(2,1)S(1)}, bf16[512,384]{1,0:T(8,128)(2,1)S(1)}, u32[]{:S(2)}, u32[]{:S(2)}) collective-permute-start(bf16[512,384]{1,0:T(8,128)(2,1)S(1)} %get-tuple-element.25), channel_id=1, source_target_pairs={{0,8},{1,9},{2,10},{3,11},{4,12},{5,13},{6,14},{7,15},{8,0},{9,1},... | collective-permute-start | bytes 1179656 | tf_op jit(solution)/shard_map/ppermute | solution.py:38
  71.5 7.9 %collective-permute-start.12 = (bf16[1024,128]{1,0:T(8,128)(2,1)S(1)}, bf16[1024,128]{1,0:T(8,128)(2,1)S(1)}, u32[]{:S(2)}, u32[]{:S(2)}) collective-permute-start(bf16[1024,128]{1,0:T(8,128)(2,1)S(1)} %regroup.7.refs_6_.refs_0_.refs_1_), channel_id=1, source_target_pairs={{0,1},{1,0},{2,3},{3,2},{4,5},{5,4},{6,7},{7,6},{8,9},{9,8},{10,11... | collective-permute-start | bytes 786440 | tf_op jit(solution)/shard_map/ppermute | solution.py:38
  72.7 34.2 %collective-permute-start.14 = (bf16[1024,256]{1,0:T(8,128)(2,1)S(1)}, bf16[1024,256]{1,0:T(8,128)(2,1)S(1)}, u32[]{:S(2)}, u32[]{:S(2)}) collective-permute-start(bf16[1024,256]{1,0:T(8,128)(2,1)S(1)} %regroup.9.refs_7_), channel_id=1, source_target_pairs={{0,4},{1,5},{2,6},{3,7},{4,0},{5,1},{6,2},{7,3},{8,12},{9,13},{10,... | collective-permute-start | bytes 1572872 | tf_op jit(solution)/shard_map/ppermute | solution.py:38
  74.8 6.4 %copy-start.6 = (bf16[1024,256]{1,0:T(8,128)(2,1)}, bf16[1024,256]{1,0:T(8,128)(2,1)S(1)}, u32[]{:S(2)}) copy-start(bf16[1024,256]{1,0:T(8,128)(2,1)S(1)} %regroup.11.refs_5_) | copy-start | bytes 1572868
  74.8 32.1 %collective-permute-start.15 = (bf16[1024,256]{1,0:T(8,128)(2,1)S(1)}, bf16[1024,256]{1,0:T(8,128)(2,1)S(1)}, u32[]{:S(2)}, u32[]{:S(2)}) collective-permute-start(bf16[1024,256]{1,0:T(8,128)(2,1)S(1)} %regroup.11.refs_5_), channel_id=1, source_target_pairs={{0,2},{1,3},{2,4},{3,5},{4,6},{5,7},{6,0},{7,1},{8,10},{9,11},{10,... | collective-permute-start | bytes 1572872 | tf_op jit(solution)/shard_map/ppermute | solution.py:38
  75.5 31.4 %collective-permute-start.16 = (bf16[1024,256]{1,0:T(8,128)(2,1)S(1)}, bf16[1024,256]{1,0:T(8,128)(2,1)S(1)}, u32[]{:S(2)}, u32[]{:S(2)}) collective-permute-start(bf16[1024,256]{1,0:T(8,128)(2,1)S(1)} %regroup.11.refs_5_), channel_id=1, source_target_pairs={{0,6},{1,7},{2,0},{3,1},{4,2},{5,3},{6,4},{7,5},{8,14},{9,15},{10,... | collective-permute-start | bytes 1572872 | tf_op jit(solution)/shard_map/ppermute | solution.py:38
  76.3 33.6 %collective-permute-start.17 = (bf16[1024,256]{1,0:T(8,128)(2,1)S(1)}, bf16[1024,256]{1,0:T(8,128)(2,1)S(1)}, u32[]{:S(2)}, u32[]{:S(2)}) collective-permute-start(bf16[1024,256]{1,0:T(8,128)(2,1)S(1)} %regroup.11.refs_5_), channel_id=1, source_target_pairs={{0,4},{1,5},{2,6},{3,7},{4,0},{5,1},{6,2},{7,3},{8,12},{9,13},{10,... | collective-permute-start | bytes 1572872 | tf_op jit(solution)/shard_map/ppermute | solution.py:38
  77.8 15.9 %copy-start.8 = (bf16[1024,128]{1,0:T(8,128)(2,1)}, bf16[1024,128]{1,0:T(8,128)(2,1)S(1)}, u32[]{:S(2)}) copy-start(bf16[1024,128]{1,0:T(8,128)(2,1)S(1)} %regroup.10.refs_0_.refs_2_) | copy-start | bytes 786436
  79.4 14.3 %collective-permute-start.13 = (bf16[1024,128]{1,0:T(8,128)(2,1)S(1)}, bf16[1024,128]{1,0:T(8,128)(2,1)S(1)}, u32[]{:S(2)}, u32[]{:S(2)}) collective-permute-start(bf16[1024,128]{1,0:T(8,128)(2,1)S(1)} %regroup.10.refs_0_.refs_2_), channel_id=1, source_target_pairs={{0,1},{1,0},{2,3},{3,2},{4,5},{5,4},{6,7},{7,6},{8,9},{9,8},{10,11... | collective-permute-start | bytes 786440 | tf_op jit(solution)/shard_map/ppermute | solution.py:38
  136.0 48.2 %copy-start.12 = (bf16[512,512]{1,0:T(8,128)(2,1)S(1)}, bf16[512,512]{1,0:T(8,128)(2,1)}, u32[]{:S(2)}) copy-start(bf16[512,512]{1,0:T(8,128)(2,1)} %constant.90.clone.place_ref) | copy-start | bytes 1572868
  179.6 4.6 %collective-permute-start.18 = (bf16[64,64,128]{2,1,0:T(8,128)(2,1)S(1)}, bf16[64,64,128]{2,1,0:T(8,128)(2,1)S(1)}, u32[]{:S(2)}, u32[]{:S(2)}) collective-permute-start(bf16[64,64,128]{2,1,0:T(8,128)(2,1)S(1)} %all_to_all.11.own_ref), channel_id=1, source_target_pairs={{0,8},{1,9},{2,10},{3,11},{4,12},{5,13},{6,14},{7,15},{8,0},{9,1},... | collective-permute-start | bytes 3145736 | tf_op jit(solution)/shard_map/ppermute | solution.py:38
  (14 other events, 24.4 us)

commit v2 on v1

--- a/solution.py
+++ b/solution.py
@@ -243,7 +243,7 @@
         ),
         out_shape=out_shape,
         input_output_aliases=aliases,
-        compiler_params=pltpu.CompilerParams(vmem_limit_bytes=56 << 20),
+        compiler_params=pltpu.CompilerParams(vmem_limit_bytes=36 << 20),
         name="attention",
     )(*prefetch, *operands)
 
@@ -501,7 +501,8 @@
     carry = attention(q2, [*kv1[:3], kv2[0]], carry, fresh=True, blocks=(2, 1))
     q_all = [q1[0], q2[0], q1[1], q2[1]]
     place = jnp.stack([coordinate[axis] for axis in ("xl", "xh", "z", "c")])
-    parts = attention(q_all, [kv1[3], *kv2[1:]], carry, last=(place, w))
+    carry = attention(q_all, [kv1[3]], carry)
+    parts = attention(q_all, kv2[1:], carry, last=(place, w))
     parts = parts.reshape(-1, PAYLOAD, 128)
     parts = lax.all_to_all(parts, SEQ + ("xl",), split_axis=0, concat_axis=0, tiled=True)
     tile = combine(parts, noisy, 64)

time: 200 us -> 189 us (0.945)
  Pallas kernels: 82.2 us -> 73.2 us
    pallas_call x3 -> x4, Pallas kernels: 50.4 us -> 43.4 us  [attention(): pl.pallas_call(functools.partial(attention_kernel, bk, len(qs), len(kvs),...]
    unnamed x56 -> x30, local copies, waits for them, and re-layouts: 8.31 us -> 6.64 us
  transfers between devices with their start and end apart: 19 -> 19, of which waited for: 6 -> 6; matrix products, arithmetic and copies ran while one was open for 3% -> 4% of each run, Pallas kernels for 17% -> 18%
where the time goes in v2:
time: 189 us; the launch traced here: 188 us
  Pallas kernels  73.2 us (39%)
  blocking collectives  41 us (22%)
  waiting for transfers between devices  30.1 us (16%)
  starting transfers between devices  28.8 us (15%)
  local copies, waits for them, and re-layouts  11.2 us (6%)
    pallas_call x4, Pallas kernels, attention(): pl.pallas_call(functools.partial(attention_kernel, bk, len(qs), len(kvs),...  43.4 us
    ppermute x19, waiting for transfers between devices, shift(): return lax.ppermute(x, AXES, pairs)  30.1 us
    ppermute x19, starting transfers between devices, shift(): return lax.ppermute(x, AXES, pairs)  28.8 us
    all_to_all x1, blocking collectives, body(): lax.all_to_all(tile, ('xh', 'z', 'y', 'xl'), split_axis=0, concat_axis=0,...  23.1 us
    all_to_all x1, blocking collectives, body(): lax.all_to_all(parts, SEQ + ('xl',), split_axis=0, concat_axis=0, tiled=T...  17.9 us
    pallas_call x2, Pallas kernels, project(): pl.pallas_call(functools.partial(project_kernel, q_order, scale, len(afte...  13.7 us
    pallas_call x1, Pallas kernels, decode(): pl.pallas_call(decode_kernel, grid_spec=pltpu.PrefetchScalarGridSpec(num_...  12 us
    unnamed x30, local copies, waits for them, and re-layouts  6.64 us
  transfers between devices with their start and end apart: 19, of which 6 were waited for; matrix products, arithmetic and copies ran while one was open for 4% of the time, Pallas kernels for 18%

profile of v2, /device:TPU:9, one launch (start us, length us, event | category | flops | bytes accessed | tf_op | source)
XLA Modules:
  0.0 187.5 jit_solution(11959848015034415594)
XLA Ops:
  0.7 1.6 collective-permute-start
  2.3 2.1 %collective-permute-start.1 = (bf16[128,3072]{1,0:T(8,128)(2,1)}, bf16[128,3072]{1,0:T(8,128)(2,1)S(1)}, u32[]{:S(2)}, u32[]{:S(2)}) collective-permute-start(bf16[128,3072]{1,0:T(8,128)(2,1)} %refs_0_.1), channel_id=1, source_target_pairs={{0,48},{1,49},{2,50},{3,51},{4,52},{5,53},{6,54},{7,55},{8,56},{9,... | collective-permute-start | bytes 2359304 | tf_op jit(solution)/shard_map/ppermute | solution.py:38
  4.4 2.7 %collective-permute-start.2 = (bf16[128,3072]{1,0:T(8,128)(2,1)}, bf16[128,3072]{1,0:T(8,128)(2,1)S(1)}, u32[]{:S(2)}, u32[]{:S(2)}) collective-permute-start(bf16[128,3072]{1,0:T(8,128)(2,1)} %refs_0_.1), channel_id=1, source_target_pairs={{0,64},{1,65},{2,66},{3,67},{4,68},{5,69},{6,70},{7,71},{8,72},{9,... | collective-permute-start | bytes 2359304 | tf_op jit(solution)/shard_map/ppermute | solution.py:38
  7.2 1.2 collective-permute-start.8
  8.4 1.2 copy.21
  10.4 12.0 %collective-permute-done.refs_0_.refs_1_.refs_8_.refs_9_ = bf16[128,3072]{1,0:T(8,128)(2,1)S(1)} collective-permute-done((bf16[128,3072]{1,0:T(8,128)(2,1)}, bf16[128,3072]{1,0:T(8,128)(2,1)S(1)}, u32[]{:S(2)}, u32[]{:S(2)}) %collective-permute-start) | collective-permute-done | bytes 786464 | tf_op jit(solution)/shard_map/ppermute | solution.py:38
  22.5 2.3 %collective-permute-done.2.refs_2_.refs_3_.refs_4_.refs_5_ = bf16[128,3072]{1,0:T(8,128)(2,1)S(1)} collective-permute-done((bf16[128,3072]{1,0:T(8,128)(2,1)}, bf16[128,3072]{1,0:T(8,128)(2,1)S(1)}, u32[]{:S(2)}, u32[]{:S(2)}) %collective-permute-start.2) | collective-permute-done | bytes 786464 | tf_op jit(solution)/shard_map/ppermute | solution.py:38
  24.8 1.6 regroup.6
  27.5 7.1 %project.2 = (bf16[512,128]{1,0:T(8,128)(2,1)S(1)}, bf16[512,256]{1,0:T(8,128)(2,1)S(1)}, bf16[512,384]{1,0:T(8,128)(2,1)}) custom-call(bf16[128,3072]{1,0:T(8,128)(2,1)S(1)} %copy-done.5, bf16[128,3072]{1,0:T(8,128)(2,1)S(1)} %collective-permute-done.refs_0_.refs_1_.refs_8_.refs_9_, ...), custom_call_target="tpu_custom_call" | custom-call | tf_op jit(solution)/shard_map/project/pallas_call | solution.py:110
  35.3 2.2 %collective-permute-start.4 = (bf16[512,384]{1,0:T(8,128)(2,1)}, bf16[512,384]{1,0:T(8,128)(2,1)S(1)}, u32[]{:S(2)}, u32[]{:S(2)}) collective-permute-start(bf16[512,384]{1,0:T(8,128)(2,1)} %get-tuple-element.22), channel_id=1, source_target_pairs={{0,8},{1,9},{2,10},{3,11},{4,12},{5,13},{6,14},{7,15},{8,0},{9,1},... | collective-permute-start | bytes 1179656 | tf_op jit(solution)/shard_map/ppermute | solution.py:38
  37.5 2.7 %collective-permute-start.6 = (bf16[128,3072]{1,0:T(8,128)(2,1)}, bf16[128,3072]{1,0:T(8,128)(2,1)}, u32[]{:S(2)}, u32[]{:S(2)}) collective-permute-start(bf16[128,3072]{1,0:T(8,128)(2,1)} %get-tuple-element.23), channel_id=1, source_target_pairs={{0,48},{1,49},{2,50},{3,51},{4,52},{5,53},{6,54},{7,55},{8,56},{9,... | collective-permute-start | bytes 2359304 | tf_op jit(solution)/shard_map/ppermute | solution.py:38
  40.1 2.7 %collective-permute-start.7 = (bf16[128,3072]{1,0:T(8,128)(2,1)}, bf16[128,3072]{1,0:T(8,128)(2,1)}, u32[]{:S(2)}, u32[]{:S(2)}) collective-permute-start(bf16[128,3072]{1,0:T(8,128)(2,1)} %get-tuple-element.24), channel_id=1, source_target_pairs={{0,64},{1,65},{2,66},{3,67},{4,68},{5,69},{6,70},{7,71},{8,72},{9,... | collective-permute-start | bytes 2359304 | tf_op jit(solution)/shard_map/ppermute | solution.py:38
  46.1 1.4 collective-permute-start.9
  52.4 8.1 %collective-permute-done.5.refs_4_.refs_0_ = bf16[128,3072]{1,0:T(8,128)(2,1)} collective-permute-done((bf16[128,3072]{1,0:T(8,128)(2,1)}, bf16[128,3072]{1,0:T(8,128)(2,1)}, u32[]{:S(2)}, u32[]{:S(2)}) %collective-permute-start.5) | collective-permute-done | bytes 786464 | tf_op jit(solution)/shard_map/ppermute | solution.py:38
  61.5 1.6 copy-done.2
  63.1 6.7 %project.3 = (bf16[512,128]{1,0:T(8,128)(2,1)S(1)}, bf16[512,256]{1,0:T(8,128)(2,1)S(1)}, bf16[512,384]{1,0:T(8,128)(2,1)S(1)}) custom-call(bf16[128,3072]{1,0:T(8,128)(2,1)} %collective-permute-done.5.refs_4_.refs_0_, bf16[128,3072]{1,0:T(8,128)(2,1)} %collective-permute-done.6.refs_5_.refs_1_, bf16[128,3072]{1,0:T(8,128)(2,1)} %collective-permute-done.7.refs_6_.refs_2_, ...), custom_call_target="tpu_custom_call" | custom-call | tf_op jit(solution)/shard_map/project/pallas_call | solution.py:110
  69.8 1.5 collective-permute-start.11
  71.3 1.2 collective-permute-start.12
  72.5 2.0 %collective-permute-start.17 = (bf16[1024,256]{1,0:T(8,128)(2,1)S(1)}, bf16[1024,256]{1,0:T(8,128)(2,1)S(1)}, u32[]{:S(2)}, u32[]{:S(2)}) collective-permute-start(bf16[1024,256]{1,0:T(8,128)(2,1)S(1)} %regroup.9.refs_7_), channel_id=1, source_target_pairs={{0,4},{1,5},{2,6},{3,7},{4,0},{5,1},{6,2},{7,3},{8,12},{9,13},{10,... | collective-permute-start | bytes 1572872 | tf_op jit(solution)/shard_map/ppermute | solution.py:38
  76.1 1.4 collective-permute-start.16
  77.5 1.6 collective-permute-done.12.refs_1_.refs_2_.refs_3_
  80.4 9.9 %attention.4 = (f32[4096,256]{1,0:T(8,128)S(1)}, f32[4096,128]{1,0:T(8,128)S(1)}) custom-call(bf16[1024,128]{1,0:T(8,128)(2,1)S(1)} %regroup.7.refs_6_.refs_0_.refs_1_, bf16[1024,128]{1,0:T(8,128)(2,1)S(1)} %collective-permute-done.12.refs_1_.refs_2_.refs_3_, bf16[1024,256]{1,0:T(8,128)(2,1)S(1)} %regroup.8.refs_2_, ...), custom_call_target="tpu_custom_call" | custom-call | tf_op jit(solution)/shard_map/attention/pallas_call | solution.py:234
  90.3 9.9 %attention.5 = (f32[4096,256]{1,0:T(8,128)S(1)}, f32[4096,128]{1,0:T(8,128)S(1)}) custom-call(bf16[1024,128]{1,0:T(8,128)(2,1)S(1)} %regroup.10.refs_0_.refs_1_.refs_2_, bf16[1024,128]{1,0:T(8,128)(2,1)S(1)} %collective-permute-done.13.refs_1_.refs_3_.refs_4_, bf16[1024,256]{1,0:T(8,128)(2,1)S(1)} %regroup.8.refs_2_, ...), custom_call_target="tpu_custom_call", output_to_operand_aliasing={{0}: (6, {}), {1}: (7, {})} | custom-call | tf_op jit(solution)/shard_map/attention/pallas_call | solution.py:234
  100.2 5.8 %attention.6 = (f32[4096,256]{1,0:T(8,128)S(1)}, f32[4096,128]{1,0:T(8,128)S(1)}) custom-call(bf16[1024,128]{1,0:T(8,128)(2,1)S(1)} %regroup.7.refs_6_.refs_0_.refs_1_, bf16[1024,128]{1,0:T(8,128)(2,1)S(1)} %regroup.10.refs_0_.refs_1_.refs_2_, ...), custom_call_target="tpu_custom_call", output_to_operand_aliasing={{0}: (5, {}), {1}: (6, {})} | custom-call | tf_op jit(solution)/shard_map/attention/pallas_call | solution.py:234
  106.0 3.6 %collective-permute-done.16.refs_7_ = bf16[1024,256]{1,0:T(8,128)(2,1)S(1)} collective-permute-done((bf16[1024,256]{1,0:T(8,128)(2,1)S(1)}, bf16[1024,256]{1,0:T(8,128)(2,1)S(1)}, u32[]{:S(2)}, u32[]{:S(2)}) %collective-permute-start.16) | collective-permute-done | bytes 524320 | tf_op jit(solution)/shard_map/ppermute | solution.py:38
  109.7 17.9 %attention.7 = bf16[2,4,2,2,80,128]{5,4,3,2,1,0:T(8,128)(2,1)S(1)} custom-call(s32[4]{0:T(128)S(1)} %pad_add_fusion.1.refs_0_, bf16[1024,128]{1,0:T(8,128)(2,1)S(1)} %regroup.7.refs_6_.refs_0_.refs_1_, bf16[1024,128]{1,0:T(8,128)(2,1)S(1)} %regroup.10.refs_0_.refs_1_.refs_2_, bf16[1024,128]{1,0:T(8,128)(2,1)S(1)} %collective-permute-done.12.refs_1_.refs_2_.refs_3_, ...), custom_call_target="tpu_custom_call" | custom-call | tf_op jit(solution)/shard_map/attention/pallas_call | solution.py:234
  127.6 17.9 %all_to_all.10.parts_ref = bf16[32,80,128]{2,1,0:T(8,128)(2,1)} all-to-all(bf16[32,80,128]{2,1,0:T(8,128)(2,1)S(1)} %bitcast.24), channel_id=1, replica_groups=mesh['xh'=2,'z'=4,'c'=2,'y'=4,'xl'=2] {'xh','z','c','xl'}, dimensions={0} | all-to-all | bytes 1310720 | tf_op jit(solution)/shard_map/all_to_all | solution.py:507
  145.4 2.3 %latent_tile.1 = bf16[64,64,128]{2,1,0:T(8,128)(2,1)} custom-call(bf16[32,80,128]{2,1,0:T(8,128)(2,1)} %all_to_all.10.parts_ref, f32[64,128]{1,0:T(8,128)} %bitcast.26), custom_call_target="tpu_custom_call" | custom-call | tf_op jit(solution)/shard_map/latent_tile/pallas_call | solution.py:270
  147.8 23.1 %all_to_all.11.own_ref = bf16[64,64,128]{2,1,0:T(8,128)(2,1)S(1)} all-to-all(bf16[64,64,128]{2,1,0:T(8,128)(2,1)} %latent_tile.1), channel_id=1, replica_groups=mesh['xh'=2,'z'=4,'c'=2,'y'=4,'xl'=2] {'xh','z','y','xl'}, dimensions={0} | all-to-all | bytes 2097152 | tf_op jit(solution)/shard_map/all_to_all | solution.py:510
  170.9 2.3 %collective-permute-start.18 = (bf16[64,64,128]{2,1,0:T(8,128)(2,1)S(1)}, bf16[64,64,128]{2,1,0:T(8,128)(2,1)S(1)}, u32[]{:S(2)}, u32[]{:S(2)}) collective-permute-start(bf16[64,64,128]{2,1,0:T(8,128)(2,1)S(1)} %all_to_all.11.own_ref), channel_id=1, source_target_pairs={{0,8},{1,9},{2,10},{3,11},{4,12},{5,13},{6,14},{7,15},{8,0},{9,1},... | collective-permute-start | bytes 3145736 | tf_op jit(solution)/shard_map/ppermute | solution.py:38
  173.2 2.3 %collective-permute-done.18.other_ref = bf16[64,64,128]{2,1,0:T(8,128)(2,1)S(1)} collective-permute-done((bf16[64,64,128]{2,1,0:T(8,128)(2,1)S(1)}, bf16[64,64,128]{2,1,0:T(8,128)(2,1)S(1)}, u32[]{:S(2)}, u32[]{:S(2)}) %collective-permute-start.18) | collective-permute-done | bytes 1048608 | tf_op jit(solution)/shard_map/ppermute | solution.py:38
  175.5 12.0 %decode.1 = bf16[1,4,512,2048]{3,2,1,0:T(8,128)(2,1)} custom-call(s32[17]{0:T(128)S(1)} %copy-done.11, bf16[64,64,128]{2,1,0:T(8,128)(2,1)S(1)} %all_to_all.11.own_ref, bf16[64,64,128]{2,1,0:T(8,128)(2,1)S(1)} %collective-permute-done.18.other_ref, bf16[512,512]{1,0:T(8,128)(2,1)S(1)} %copy-done.6, ...), custom_call_target="tpu_custom_call" | custom-call | tf_op jit(solution)/shard_map/decode/pallas_call | solution.py:392
  (72 shorter events, 13.9 us)
Async XLA Ops:
  0.0 48.2 %copy-start = (bf16[2048,64]{0,1:T(8,128)(2,1)S(1)}, bf16[2048,64]{0,1:T(8,128)(2,1)}, u32[]{:S(2)}) copy-start(bf16[2048,64]{0,1:T(8,128)(2,1)} %param.13) | copy-start | bytes 786436
  0.0 26.4 %collective-permute-start.3 = (bf16[3,3072,128]{2,1,0:T(8,128)(2,1)}, bf16[3,3072,128]{2,1,0:T(8,128)(2,1)}, u32[]{:S(2)}, u32[]{:S(2)}) collective-permute-start(bf16[3,3072,128]{2,1,0:T(8,128)(2,1)} %refs_4_.3), channel_id=1, source_target_pairs={{0,8},{1,9},{2,10},{3,11},{4,12},{5,13},{6,14},{7,15},{8,0},{9,1},... | collective-permute-start | bytes 7077896 | tf_op jit(solution)/shard_map/ppermute | solution.py:38
  0.7 21.8 %collective-permute-start = (bf16[128,3072]{1,0:T(8,128)(2,1)}, bf16[128,3072]{1,0:T(8,128)(2,1)S(1)}, u32[]{:S(2)}, u32[]{:S(2)}) collective-permute-start(bf16[128,3072]{1,0:T(8,128)(2,1)} %refs_0_.1), channel_id=1, source_target_pairs={{0,16},{1,17},{2,18},{3,19},{4,20},{5,21},{6,22},{7,23},{8,24},{9,... | collective-permute-start | bytes 2359304 | tf_op jit(solution)/shard_map/ppermute | solution.py:38
  2.3 20.2 %collective-permute-start.1 = (bf16[128,3072]{1,0:T(8,128)(2,1)}, bf16[128,3072]{1,0:T(8,128)(2,1)S(1)}, u32[]{:S(2)}, u32[]{:S(2)}) collective-permute-start(bf16[128,3072]{1,0:T(8,128)(2,1)} %refs_0_.1), channel_id=1, source_target_pairs={{0,48},{1,49},{2,50},{3,51},{4,52},{5,53},{6,54},{7,55},{8,56},{9,... | collective-permute-start | bytes 2359304 | tf_op jit(solution)/shard_map/ppermute | solution.py:38
  4.4 20.4 %collective-permute-start.2 = (bf16[128,3072]{1,0:T(8,128)(2,1)}, bf16[128,3072]{1,0:T(8,128)(2,1)S(1)}, u32[]{:S(2)}, u32[]{:S(2)}) collective-permute-start(bf16[128,3072]{1,0:T(8,128)(2,1)} %refs_0_.1), channel_id=1, source_target_pairs={{0,64},{1,65},{2,66},{3,67},{4,68},{5,69},{6,70},{7,71},{8,72},{9,... | collective-permute-start | bytes 2359304 | tf_op jit(solution)/shard_map/ppermute | solution.py:38
  7.2 39.0 %collective-permute-start.8 = (bf16[128,3072]{1,0:T(8,128)(2,1)}, bf16[128,3072]{1,0:T(8,128)(2,1)}, u32[]{:S(2)}, u32[]{:S(2)}) collective-permute-start(bf16[128,3072]{1,0:T(8,128)(2,1)} %refs_0_.1), channel_id=1, source_target_pairs={{0,96},{1,97},{2,98},{3,99},{4,100},{5,101},{6,102},{7,103},{8,104... | collective-permute-start | bytes 2359304 | tf_op jit(solution)/shard_map/ppermute | solution.py:38
  24.8 2.5 %copy-start.1 = (bf16[3,3072,128]{2,1,0:T(8,128)(2,1)S(1)}, bf16[3,3072,128]{2,1,0:T(8,128)(2,1)}, u32[]{:S(2)}) copy-start(bf16[3,3072,128]{2,1,0:T(8,128)(2,1)} %refs_4_.3) | copy-start | bytes 7077892
  24.8 2.7 %copy-start.5 = (bf16[128,3072]{1,0:T(8,128)(2,1)S(1)}, bf16[128,3072]{1,0:T(8,128)(2,1)}, u32[]{:S(2)}) copy-start(bf16[128,3072]{1,0:T(8,128)(2,1)} %refs_0_.1) | copy-start | bytes 2359300
  27.5 15.4 %copy-start.13 = (s32[128]{0:T(128)S(1)}, s32[128]{0:T(128)}, u32[]{:S(2)}) copy-start(s32[128]{0:T(128)} %param.17) | copy-start | bytes 1540
  27.5 16.9 %copy-start.12 = (s32[256,4]{0,1:T(4,128)S(1)}, s32[256,4]{0,1:T(4,128)}, u32[]{:S(2)}) copy-start(s32[256,4]{0,1:T(4,128)} %param.18) | copy-start | bytes 12292
  35.3 13.7 %copy-start.3 = (bf16[512,256]{1,0:T(8,128)(2,1)}, bf16[512,256]{1,0:T(8,128)(2,1)S(1)}, u32[]{:S(2)}) copy-start(bf16[512,256]{1,0:T(8,128)(2,1)S(1)} %get-tuple-element.25.refs_0_) | copy-start | bytes 786436
  35.3 10.6 %collective-permute-start.4 = (bf16[512,384]{1,0:T(8,128)(2,1)}, bf16[512,384]{1,0:T(8,128)(2,1)S(1)}, u32[]{:S(2)}, u32[]{:S(2)}) collective-permute-start(bf16[512,384]{1,0:T(8,128)(2,1)} %get-tuple-element.22), channel_id=1, source_target_pairs={{0,8},{1,9},{2,10},{3,11},{4,12},{5,13},{6,14},{7,15},{8,0},{9,1},... | collective-permute-start | bytes 1179656 | tf_op jit(solution)/shard_map/ppermute | solution.py:38
  37.5 23.0 %collective-permute-start.5 = (bf16[128,3072]{1,0:T(8,128)(2,1)}, bf16[128,3072]{1,0:T(8,128)(2,1)}, u32[]{:S(2)}, u32[]{:S(2)}) collective-permute-start(bf16[128,3072]{1,0:T(8,128)(2,1)} %get-tuple-element.20.refs_6_), channel_id=1, source_target_pairs={{0,16},{1,17},{2,18},{3,19},{4,20},{5,21},{6,22},{7,23},{8,24},{9,... | collective-permute-start | bytes 2359304 | tf_op jit(solution)/shard_map/ppermute | solution.py:38
  37.5 23.0 %collective-permute-start.6 = (bf16[128,3072]{1,0:T(8,128)(2,1)}, bf16[128,3072]{1,0:T(8,128)(2,1)}, u32[]{:S(2)}, u32[]{:S(2)}) collective-permute-start(bf16[128,3072]{1,0:T(8,128)(2,1)} %get-tuple-element.23), channel_id=1, source_target_pairs={{0,48},{1,49},{2,50},{3,51},{4,52},{5,53},{6,54},{7,55},{8,56},{9,... | collective-permute-start | bytes 2359304 | tf_op jit(solution)/shard_map/ppermute | solution.py:38
  40.1 20.4 %collective-permute-start.7 = (bf16[128,3072]{1,0:T(8,128)(2,1)}, bf16[128,3072]{1,0:T(8,128)(2,1)}, u32[]{:S(2)}, u32[]{:S(2)}) collective-permute-start(bf16[128,3072]{1,0:T(8,128)(2,1)} %get-tuple-element.24), channel_id=1, source_target_pairs={{0,64},{1,65},{2,66},{3,67},{4,68},{5,69},{6,70},{7,71},{8,72},{9,... | collective-permute-start | bytes 2359304 | tf_op jit(solution)/shard_map/ppermute | solution.py:38
  45.9 14.6 %collective-permute-start.10 = (bf16[1024,256]{1,0:T(8,128)(2,1)S(1)}, bf16[1024,256]{1,0:T(8,128)(2,1)S(1)}, u32[]{:S(2)}, u32[]{:S(2)}) collective-permute-start(bf16[1024,256]{1,0:T(8,128)(2,1)S(1)} %regroup.8.refs_2_), channel_id=1, source_target_pairs={{0,6},{1,7},{2,0},{3,1},{4,2},{5,3},{6,4},{7,5},{8,14},{9,15},{10,... | collective-permute-start | bytes 1572872 | tf_op jit(solution)/shard_map/ppermute | solution.py:38
  46.1 14.4 %collective-permute-start.9 = (bf16[1024,256]{1,0:T(8,128)(2,1)S(1)}, bf16[1024,256]{1,0:T(8,128)(2,1)S(1)}, u32[]{:S(2)}, u32[]{:S(2)}) collective-permute-start(bf16[1024,256]{1,0:T(8,128)(2,1)S(1)} %regroup.8.refs_2_), channel_id=1, source_target_pairs={{0,2},{1,3},{2,4},{3,5},{4,6},{5,7},{6,0},{7,1},{8,10},{9,11},{10,... | collective-permute-start | bytes 1572872 | tf_op jit(solution)/shard_map/ppermute | solution.py:38
  50.6 10.9 %copy-start.7 = (f32[128,16,4]{0,1,2:T(8,128)}, f32[128,16,4]{0,1,2:T(8,128)S(1)}, u32[]{:S(2)}) copy-start(f32[128,16,4]{0,1,2:T(8,128)S(1)} %copy.23) | copy-start | bytes 98308
  51.4 10.1 %copy-start.10 = (s32[17]{0:T(128)}, s32[17]{0:T(128)S(1)}, u32[]{:S(2)}) copy-start(s32[17]{0:T(128)S(1)} %pad_add_fusion.refs_8_.ids_ref) | copy-start | bytes 208
  51.4 0.9 copy-start.9
  60.5 1.0 copy-start.4
  61.5 1.7 copy-start.2
  69.8 4.7 %collective-permute-start.11 = (bf16[512,384]{1,0:T(8,128)(2,1)S(1)}, bf16[512,384]{1,0:T(8,128)(2,1)S(1)}, u32[]{:S(2)}, u32[]{:S(2)}) collective-permute-start(bf16[512,384]{1,0:T(8,128)(2,1)S(1)} %get-tuple-element.27), channel_id=1, source_target_pairs={{0,8},{1,9},{2,10},{3,11},{4,12},{5,13},{6,14},{7,15},{8,0},{9,1},... | collective-permute-start | bytes 1179656 | tf_op jit(solution)/shard_map/ppermute | solution.py:38
  71.3 7.9 %collective-permute-start.12 = (bf16[1024,128]{1,0:T(8,128)(2,1)S(1)}, bf16[1024,128]{1,0:T(8,128)(2,1)S(1)}, u32[]{:S(2)}, u32[]{:S(2)}) collective-permute-start(bf16[1024,128]{1,0:T(8,128)(2,1)S(1)} %regroup.7.refs_6_.refs_0_.refs_1_), channel_id=1, source_target_pairs={{0,1},{1,0},{2,3},{3,2},{4,5},{5,4},{6,7},{7,6},{8,9},{9,8},{10,11... | collective-permute-start | bytes 786440 | tf_op jit(solution)/shard_map/ppermute | solution.py:38
  72.5 27.7 %collective-permute-start.17 = (bf16[1024,256]{1,0:T(8,128)(2,1)S(1)}, bf16[1024,256]{1,0:T(8,128)(2,1)S(1)}, u32[]{:S(2)}, u32[]{:S(2)}) collective-permute-start(bf16[1024,256]{1,0:T(8,128)(2,1)S(1)} %regroup.9.refs_7_), channel_id=1, source_target_pairs={{0,4},{1,5},{2,6},{3,7},{4,0},{5,1},{6,2},{7,3},{8,12},{9,13},{10,... | collective-permute-start | bytes 1572872 | tf_op jit(solution)/shard_map/ppermute | solution.py:38
  74.6 31.5 %collective-permute-start.14 = (bf16[1024,256]{1,0:T(8,128)(2,1)S(1)}, bf16[1024,256]{1,0:T(8,128)(2,1)S(1)}, u32[]{:S(2)}, u32[]{:S(2)}) collective-permute-start(bf16[1024,256]{1,0:T(8,128)(2,1)S(1)} %regroup.11.refs_5_), channel_id=1, source_target_pairs={{0,2},{1,3},{2,4},{3,5},{4,6},{5,7},{6,0},{7,1},{8,10},{9,11},{10,... | collective-permute-start | bytes 1572872 | tf_op jit(solution)/shard_map/ppermute | solution.py:38
  75.4 30.6 %collective-permute-start.15 = (bf16[1024,256]{1,0:T(8,128)(2,1)S(1)}, bf16[1024,256]{1,0:T(8,128)(2,1)S(1)}, u32[]{:S(2)}, u32[]{:S(2)}) collective-permute-start(bf16[1024,256]{1,0:T(8,128)(2,1)S(1)} %regroup.11.refs_5_), channel_id=1, source_target_pairs={{0,6},{1,7},{2,0},{3,1},{4,2},{5,3},{6,4},{7,5},{8,14},{9,15},{10,... | collective-permute-start | bytes 1572872 | tf_op jit(solution)/shard_map/ppermute | solution.py:38
  76.1 33.6 %collective-permute-start.16 = (bf16[1024,256]{1,0:T(8,128)(2,1)S(1)}, bf16[1024,256]{1,0:T(8,128)(2,1)S(1)}, u32[]{:S(2)}, u32[]{:S(2)}) collective-permute-start(bf16[1024,256]{1,0:T(8,128)(2,1)S(1)} %regroup.11.refs_5_), channel_id=1, source_target_pairs={{0,4},{1,5},{2,6},{3,7},{4,0},{5,1},{6,2},{7,3},{8,12},{9,13},{10,... | collective-permute-start | bytes 1572872 | tf_op jit(solution)/shard_map/ppermute | solution.py:38
  79.1 11.2 %collective-permute-start.13 = (bf16[1024,128]{1,0:T(8,128)(2,1)S(1)}, bf16[1024,128]{1,0:T(8,128)(2,1)S(1)}, u32[]{:S(2)}, u32[]{:S(2)}) collective-permute-start(bf16[1024,128]{1,0:T(8,128)(2,1)S(1)} %regroup.10.refs_0_.refs_1_.refs_2_), channel_id=1, source_target_pairs={{0,1},{1,0},{2,3},{3,2},{4,5},{5,4},{6,7},{7,6},{8,9},{9,8},{10,11... | collective-permute-start | bytes 786440 | tf_op jit(solution)/shard_map/ppermute | solution.py:38
  127.5 48.0 %copy-start.6 = (bf16[512,512]{1,0:T(8,128)(2,1)S(1)}, bf16[512,512]{1,0:T(8,128)(2,1)}, u32[]{:S(2)}) copy-start(bf16[512,512]{1,0:T(8,128)(2,1)} %constant.90.clone.place_ref) | copy-start | bytes 1572868
  127.5 48.0 %copy-start.11 = (s32[17]{0:T(128)S(1)}, s32[17]{0:T(128)}, u32[]{:S(2)}) copy-start(s32[17]{0:T(128)} %copy-done.10) | copy-start | bytes 208
  170.9 4.6 %collective-permute-start.18 = (bf16[64,64,128]{2,1,0:T(8,128)(2,1)S(1)}, bf16[64,64,128]{2,1,0:T(8,128)(2,1)S(1)}, u32[]{:S(2)}, u32[]{:S(2)}) collective-permute-start(bf16[64,64,128]{2,1,0:T(8,128)(2,1)S(1)} %all_to_all.11.own_ref), channel_id=1, source_target_pairs={{0,8},{1,9},{2,10},{3,11},{4,12},{5,13},{6,14},{7,15},{8,0},{9,1},... | collective-permute-start | bytes 3145736 | tf_op jit(solution)/shard_map/ppermute | solution.py:38
  (1 other events, 0.7 us)
